TPU v7x, 256 devices: a whole 4x4x8 slice. The times are simulated.
256 devices in a mesh: tx: 4 (over x), ty: 4 (over y), tz: 16 (over z, core).
Axes of the slice: x: 4, y: 4, z: 8, core: 2. Of those that a mesh axis runs over, the one named last changes fastest.
Arguments:
- surface: float32 [4, 4, 16, 4, 3, 312], P('tx', 'ty', 'tz'), may hold values from -6 to 6
- synthesis: float32 [312, 169], replicated, may hold values from -0.5 to 0.5
- analysis: float32 [169, 312], replicated, may hold values from -0.3125 to 0.3125
- stiffness: float32 [169], replicated, may hold values from 0.1 to 10
- upsample: float32 [1248, 312], replicated, may hold values from -0.3125 to 0.3125
- quad_weight: float32 [1248], replicated, may hold values from 0.5 to 2
- near_pairs: int32 [4, 4, 16, 16, 3], P('tx', 'ty', 'tz'), may hold values from 0 to 26, as said below
- pair_count: int32 [4, 4, 16], P('tx', 'ty', 'tz'), may hold values from 1 to 16, as said below
Outputs:
- velocity: float32 [4, 4, 16, 4, 3, 312], P('tx', 'ty', 'tz')
Inputs may be any that keep to these rules, and one draw needn't show every extreme that they name: `near_pairs`: column 0 and column 2 name cells 0 to 3; column 1 names a neighbour tile code 0 to 26 whose tile lies inside the mesh; when the code is 13 the two cells differ. `pair_count`: some tile uses all 16 slots.
All inputs are finite; a program needn't handle non-finite values.
Results may differ from a plain program's by a relative error of at most 0.0001.
Values sent between devices are 32-bit elements; how exact they have to be, the bound alone decides.
A program may use at most 64 MiB of HBM per device.

v0:
```python
import math

import jax
import jax.numpy as jnp
from jax import lax
from jax.sharding import PartitionSpec as P

smooth_sq = 0.25


def with_halo(block, sides, width):
    for axis, dim in sides:
        count = lax.axis_size(axis)
        forward = [(i, i + 1) for i in range(count - 1)]
        backward = [(target, source) for source, target in forward]
        low = lax.ppermute(
            lax.slice_in_dim(block, block.shape[dim] - width, None, axis=dim), axis, forward
        )
        high = lax.ppermute(lax.slice_in_dim(block, 0, width, axis=dim), axis, backward)
        block = jnp.concatenate([low, block, high], axis=dim)
    return block


def stokes_velocity(targets, sources, density, quad_weight):
    blocks = 3
    block_width = sources.shape[-1] // blocks
    source_blocks = jnp.moveaxis(sources.reshape(3, blocks, block_width), 1, 0)
    density_blocks = jnp.moveaxis((density * quad_weight).reshape(3, blocks, block_width), 1, 0)

    def add_block(running, block_item):
        placed, weighted = block_item
        offset = targets[:, :, None] - placed[:, None, :]
        inverse = 1.0 / jnp.sqrt(jnp.sum(offset * offset, axis=0) + smooth_sq)
        along = jnp.sum(offset * weighted[:, None, :], axis=0)
        summand = weighted[:, None, :] * inverse + offset * (along * inverse**3)
        return (running + jnp.sum(summand, axis=2), None)

    running = lax.scan(
        add_block, jnp.zeros(targets.shape, jnp.float32), (source_blocks, density_blocks)
    )[0]
    return running * (1.0 / math.sqrt(sources.shape[-1]))


def raise_points(values, upsample):
    return jnp.einsum("...p,up->...u", values, upsample, precision=lax.Precision.HIGHEST)


def shards(surface, synthesis, analysis, stiffness, upsample, quad_weight, near_pairs, pair_count):
    highest = lax.Precision.HIGHEST
    own_cells = surface[0, 0, 0]
    per_tile = own_cells.shape[0]
    points = own_cells.shape[-1]
    coeffs = jnp.einsum("qp,ckp->ckq", analysis, own_cells, precision=highest) * stiffness
    bend_force = jnp.einsum("pq,ckq->ckp", synthesis, coeffs, precision=highest)
    own_pos = raise_points(own_cells, upsample)
    own_den = raise_points(bend_force, upsample)
    carried = jnp.stack([own_pos, own_den], axis=1)[None, None, None]
    near_pos, near_carried = (
        with_halo(surface, (("tx", 0), ("ty", 1), ("tz", 2)), 1),
        with_halo(carried, (("tx", 0), ("ty", 1), ("tz", 2)), 1),
    )
    near_pos = near_pos.reshape(27 * per_tile, 3, points)
    near_carried = near_carried.reshape((27 * per_tile,) + near_carried.shape[4:])
    slot_table = near_pairs[0, 0, 0]
    used_count = pair_count[0, 0, 0]
    slots = slot_table.shape[0]
    own_slot = slot_table[:, 0]
    far_rows = slot_table[:, 1] * per_tile + slot_table[:, 2]
    slot_used = (jnp.arange(slots, dtype=jnp.int32) < used_count).astype(jnp.float32)

    def per_pair(pair_item):
        near_cell, far_row, weight = pair_item
        far_pos = near_pos[far_row]
        far_source = near_carried[far_row, 0]
        far_density = near_carried[far_row, 1]
        on_near = (
            stokes_velocity(own_cells[near_cell], far_source, far_density, quad_weight) * weight
        )
        on_far = (
            stokes_velocity(far_pos, own_pos[near_cell], own_den[near_cell], quad_weight) * weight
        )
        return (on_near, on_far)

    on_near, on_far = lax.map(per_pair, (own_slot, far_rows, slot_used))
    pick_near = (own_slot[None, :] == jnp.arange(per_tile, dtype=jnp.int32)[:, None]).astype(
        jnp.float32
    )
    near_sum = jnp.einsum("cs,skp->ckp", pick_near, on_near, precision=highest)
    pick_far = (far_rows[None, :] == jnp.arange(27 * per_tile, dtype=jnp.int32)[:, None]).astype(
        jnp.float32
    )
    partial_value = jnp.einsum("cs,skp->ckp", pick_far, on_far, precision=highest).reshape(
        3, 3, 3, per_tile, 3, points
    )
    extended = with_halo(partial_value, (("tx", 0), ("ty", 1), ("tz", 2)), 1)
    came_back = jnp.sum(extended[0::2, 0::2, 0::2], axis=(0, 1, 2))
    velocity = 0.25 * bend_force + near_sum + came_back
    return velocity[None, None, None]


def solution(mesh):
    return jax.shard_map(
        shards,
        mesh=mesh,
        in_specs=(
            P("tx", "ty", "tz", None, None, None),
            P(),
            P(),
            P(),
            P(),
            P(),
            P("tx", "ty", "tz", None, None),
            P("tx", "ty", "tz"),
        ),
        out_specs=P("tx", "ty", "tz", None, None, None),
        check_vma=False,
    )
```

profile of v0, /device:TPU:97, one launch (start us, length us, event | category | flops | bytes accessed | tf_op | source)
XLA Modules:
  0.0 360.0 jit_solution(17633405563524426697)
XLA Ops:
  0.0 1.4 copy-done
  1.4 1.6 fusion.12
  3.1 1.4 convolution_multiply_fusion
  5.7 3.1 collective-permute-start
  10.7 3.8 %collective-permute-done.1 = f32[1,1,1,4,2,3,1248]{6,3,5,4,2,1,0:T(4,128)S(1)} collective-permute-done((f32[1,1,1,4,2,3,1248]{6,3,5,4,2,1,0:T(4,128)S(1)}, f32[1,1,1,4,2,3,1248]{6,3,5,4,2,1,0:T(4,128)S(1)}, u32[]{:S(2)}, u32[]{:S(2)}) %collective-permute-start.1) | collective-permute-done | bytes 119840 | tf_op jit(solution)/shard_map/ppermute | solution.py:19
  14.6 3.2 collective-permute-start.2
  19.1 4.4 %collective-permute-done.2 = f32[3,1,1,4,2,3,1248]{6,3,5,4,2,1,0:T(4,128)S(1)} collective-permute-done((f32[3,1,1,4,2,3,1248]{6,3,5,4,2,1,0:T(4,128)S(1)}, f32[3,1,1,4,2,3,1248]{6,3,5,4,2,1,0:T(4,128)S(1)}, u32[]{:S(2)}, u32[]{:S(2)}) %collective-permute-start.2) | collective-permute-done | bytes 359456 | tf_op jit(solution)/shard_map/ppermute | solution.py:16
  23.5 3.9 %collective-permute-done.3 = f32[3,1,1,4,2,3,1248]{6,3,5,4,2,1,0:T(4,128)S(1)} collective-permute-done((f32[3,1,1,4,2,3,1248]{6,3,5,4,2,1,0:T(4,128)S(1)}, f32[3,1,1,4,2,3,1248]{6,3,5,4,2,1,0:T(4,128)S(1)}, u32[]{:S(2)}, u32[]{:S(2)}) %collective-permute-start.3) | collective-permute-done | bytes 359456 | tf_op jit(solution)/shard_map/ppermute | solution.py:19
  28.7 7.9 %collective-permute-start.4 = (f32[3,3,1,4,2,3,1248]{6,3,5,4,2,1,0:T(4,128)}, f32[3,3,1,4,2,3,1248]{6,3,5,4,2,1,0:T(4,128)}, u32[]{:S(2)}, u32[]{:S(2)}) collective-permute-start(f32[3,3,1,4,2,3,1248]{6,3,5,4,2,1,0:T(4,128)} %pad_maximum_fusion.2), channel_id=1, source_target_pairs={{0,1},{1,2},{2,3},{3,4},{4,5},{5,6},{6,7},{7,8},{8,9},{9,10},{10,1... | collective-permute-start | bytes 3234824 | tf_op jit(solution)/shard_map/ppermute | solution.py:16
  36.6 1.9 collective-permute-start.5
  38.6 3.1 collective-permute-start.6
  41.7 1.3 collective-permute-start.7
  43.0 3.6 collective-permute-done.7
  46.6 3.2 collective-permute-start.8
  51.1 3.6 collective-permute-done.9
  54.7 7.3 %collective-permute-start.10 = (f32[3,3,1,4,3,312]{5,3,4,2,1,0:T(4,128)S(1)}, f32[3,3,1,4,3,312]{5,3,4,2,1,0:T(4,128)}, u32[]{:S(2)}, u32[]{:S(2)}) collective-permute-start(f32[3,3,1,4,3,312]{5,3,4,2,1,0:T(4,128)S(1)} %pad_maximum_fusion.13), channel_id=1, source_target_pairs={{0,1},{1,2},{2,3},{3,4},{4,5},{5,6},{6,7},{7,8},{8,9},{9,10},{10,1... | collective-permute-start | bytes 404360 | tf_op jit(solution)/shard_map/ppermute | solution.py:16
  62.0 1.9 collective-permute-start.11
  65.3 4.7 %collective-permute-done.11 = f32[3,3,1,4,3,312]{5,3,4,2,1,0:T(4,128)} collective-permute-done((f32[3,3,1,4,3,312]{5,3,4,2,1,0:T(4,128)S(1)}, f32[3,3,1,4,3,312]{5,3,4,2,1,0:T(4,128)}, u32[]{:S(2)}, u32[]{:S(2)}) %collective-permute-start.11) | collective-permute-done | bytes 134816 | tf_op jit(solution)/shard_map/ppermute | solution.py:19
  71.3 2.1 pad_maximum_fusion
  73.4 1.7 copy.43
  75.2 3.2 copy.45
  78.3 243.1 %while.39 = (s32[]{:T(128)}, f32[16,3,312]{2,0,1:T(8,128)S(1)}, f32[16,3,312]{2,0,1:T(8,128)S(1)}, s32[16]{0:T(128)S(1)}, f32[108,2,3,1248]{3,2,1,0:T(4,128)}, /...) while((s32[]{:T(128)}, f32[16,3,312]{2,0,1:T(8,128)S(1)}, ...), condition=%wide.wide.region_11.12_spmd, body=%wide.wide.region_0.11_spmd.sunk | while | flops 8317935 | bytes 8836495 | solution.py:84
  84.7 3.7 %while.41 = (s32[]{:T(128)}, f32[3,312]{1,0:T(4,128)S(1)}, f32[3,3,416]{2,0,1:T(4,128)S(1)}, f32[1,3,312]{2,1,0:T(4,128)S(1)}, f32[3,3,416]{2,0,1:T(4,128)S(1)}, /*index=5*/s32[]{:T(128)}, s32[]{:T(128)}) while((s32[]{:T(128)}, f32[3,312]{1,0:T(4,128)S(1)}, f32[3,3,416]{2,0,1:T(4,128)S(1)}, f32[1,3,312]{2,1,0:T(4,128)S(1)}, ...), condition=%wide.region_10.10_spmd.clone, body=%wide.region_6.9_spmd.clone.sunk | while | flops 4154283 | bytes 4235803 | solution.py:38
  89.7 3.7 %while.40 = (s32[]{:T(128)}, f32[3,312]{1,0:T(4,128)S(1)}, f32[3,3,416]{2,0,1:T(4,128)S(1)}, f32[1,3,312]{2,1,0:T(4,128)S(1)}, f32[3,3,416]{2,0,1:T(4,128)S(1)}, /*index=5*/s32[]{:T(128)}, s32[]{:T(128)}) while((s32[]{:T(128)}, f32[3,312]{1,0:T(4,128)S(1)}, f32[3,3,416]{2,0,1:T(4,128)S(1)}, f32[1,3,312]{2,1,0:T(4,128)S(1)}, ...), condition=%wide.region_5.5_spmd.clone, body=%wide.region_1.4_spmd.clone.sunk | while | flops 4154283 | bytes 4235803 | solution.py:38
  99.8 3.7 %while.41 = (s32[]{:T(128)}, f32[3,312]{1,0:T(4,128)S(1)}, f32[3,3,416]{2,0,1:T(4,128)S(1)}, f32[1,3,312]{2,1,0:T(4,128)S(1)}, f32[3,3,416]{2,0,1:T(4,128)S(1)}, /*index=5*/s32[]{:T(128)}, s32[]{:T(128)}) while((s32[]{:T(128)}, f32[3,312]{1,0:T(4,128)S(1)}, f32[3,3,416]{2,0,1:T(4,128)S(1)}, f32[1,3,312]{2,1,0:T(4,128)S(1)}, ...), condition=%wide.region_10.10_spmd.clone, body=%wide.region_6.9_spmd.clone.sunk | while | flops 4154283 | bytes 4235803 | solution.py:38
  104.9 3.7 %while.40 = (s32[]{:T(128)}, f32[3,312]{1,0:T(4,128)S(1)}, f32[3,3,416]{2,0,1:T(4,128)S(1)}, f32[1,3,312]{2,1,0:T(4,128)S(1)}, f32[3,3,416]{2,0,1:T(4,128)S(1)}, /*index=5*/s32[]{:T(128)}, s32[]{:T(128)}) while((s32[]{:T(128)}, f32[3,312]{1,0:T(4,128)S(1)}, f32[3,3,416]{2,0,1:T(4,128)S(1)}, f32[1,3,312]{2,1,0:T(4,128)S(1)}, ...), condition=%wide.region_5.5_spmd.clone, body=%wide.region_1.4_spmd.clone.sunk | while | flops 4154283 | bytes 4235803 | solution.py:38
  115.0 3.7 %while.41 = (s32[]{:T(128)}, f32[3,312]{1,0:T(4,128)S(1)}, f32[3,3,416]{2,0,1:T(4,128)S(1)}, f32[1,3,312]{2,1,0:T(4,128)S(1)}, f32[3,3,416]{2,0,1:T(4,128)S(1)}, /*index=5*/s32[]{:T(128)}, s32[]{:T(128)}) while((s32[]{:T(128)}, f32[3,312]{1,0:T(4,128)S(1)}, f32[3,3,416]{2,0,1:T(4,128)S(1)}, f32[1,3,312]{2,1,0:T(4,128)S(1)}, ...), condition=%wide.region_10.10_spmd.clone, body=%wide.region_6.9_spmd.clone.sunk | while | flops 4154283 | bytes 4235803 | solution.py:38
  120.1 3.7 %while.40 = (s32[]{:T(128)}, f32[3,312]{1,0:T(4,128)S(1)}, f32[3,3,416]{2,0,1:T(4,128)S(1)}, f32[1,3,312]{2,1,0:T(4,128)S(1)}, f32[3,3,416]{2,0,1:T(4,128)S(1)}, /*index=5*/s32[]{:T(128)}, s32[]{:T(128)}) while((s32[]{:T(128)}, f32[3,312]{1,0:T(4,128)S(1)}, f32[3,3,416]{2,0,1:T(4,128)S(1)}, f32[1,3,312]{2,1,0:T(4,128)S(1)}, ...), condition=%wide.region_5.5_spmd.clone, body=%wide.region_1.4_spmd.clone.sunk | while | flops 4154283 | bytes 4235803 | solution.py:38
  130.2 3.7 %while.41 = (s32[]{:T(128)}, f32[3,312]{1,0:T(4,128)S(1)}, f32[3,3,416]{2,0,1:T(4,128)S(1)}, f32[1,3,312]{2,1,0:T(4,128)S(1)}, f32[3,3,416]{2,0,1:T(4,128)S(1)}, /*index=5*/s32[]{:T(128)}, s32[]{:T(128)}) while((s32[]{:T(128)}, f32[3,312]{1,0:T(4,128)S(1)}, f32[3,3,416]{2,0,1:T(4,128)S(1)}, f32[1,3,312]{2,1,0:T(4,128)S(1)}, ...), condition=%wide.region_10.10_spmd.clone, body=%wide.region_6.9_spmd.clone.sunk | while | flops 4154283 | bytes 4235803 | solution.py:38
  135.3 3.7 %while.40 = (s32[]{:T(128)}, f32[3,312]{1,0:T(4,128)S(1)}, f32[3,3,416]{2,0,1:T(4,128)S(1)}, f32[1,3,312]{2,1,0:T(4,128)S(1)}, f32[3,3,416]{2,0,1:T(4,128)S(1)}, /*index=5*/s32[]{:T(128)}, s32[]{:T(128)}) while((s32[]{:T(128)}, f32[3,312]{1,0:T(4,128)S(1)}, f32[3,3,416]{2,0,1:T(4,128)S(1)}, f32[1,3,312]{2,1,0:T(4,128)S(1)}, ...), condition=%wide.region_5.5_spmd.clone, body=%wide.region_1.4_spmd.clone.sunk | while | flops 4154283 | bytes 4235803 | solution.py:38
  145.4 3.7 %while.41 = (s32[]{:T(128)}, f32[3,312]{1,0:T(4,128)S(1)}, f32[3,3,416]{2,0,1:T(4,128)S(1)}, f32[1,3,312]{2,1,0:T(4,128)S(1)}, f32[3,3,416]{2,0,1:T(4,128)S(1)}, /*index=5*/s32[]{:T(128)}, s32[]{:T(128)}) while((s32[]{:T(128)}, f32[3,312]{1,0:T(4,128)S(1)}, f32[3,3,416]{2,0,1:T(4,128)S(1)}, f32[1,3,312]{2,1,0:T(4,128)S(1)}, ...), condition=%wide.region_10.10_spmd.clone, body=%wide.region_6.9_spmd.clone.sunk | while | flops 4154283 | bytes 4235803 | solution.py:38
  150.5 3.7 %while.40 = (s32[]{:T(128)}, f32[3,312]{1,0:T(4,128)S(1)}, f32[3,3,416]{2,0,1:T(4,128)S(1)}, f32[1,3,312]{2,1,0:T(4,128)S(1)}, f32[3,3,416]{2,0,1:T(4,128)S(1)}, /*index=5*/s32[]{:T(128)}, s32[]{:T(128)}) while((s32[]{:T(128)}, f32[3,312]{1,0:T(4,128)S(1)}, f32[3,3,416]{2,0,1:T(4,128)S(1)}, f32[1,3,312]{2,1,0:T(4,128)S(1)}, ...), condition=%wide.region_5.5_spmd.clone, body=%wide.region_1.4_spmd.clone.sunk | while | flops 4154283 | bytes 4235803 | solution.py:38
  160.6 3.7 %while.41 = (s32[]{:T(128)}, f32[3,312]{1,0:T(4,128)S(1)}, f32[3,3,416]{2,0,1:T(4,128)S(1)}, f32[1,3,312]{2,1,0:T(4,128)S(1)}, f32[3,3,416]{2,0,1:T(4,128)S(1)}, /*index=5*/s32[]{:T(128)}, s32[]{:T(128)}) while((s32[]{:T(128)}, f32[3,312]{1,0:T(4,128)S(1)}, f32[3,3,416]{2,0,1:T(4,128)S(1)}, f32[1,3,312]{2,1,0:T(4,128)S(1)}, ...), condition=%wide.region_10.10_spmd.clone, body=%wide.region_6.9_spmd.clone.sunk | while | flops 4154283 | bytes 4235803 | solution.py:38
  165.7 3.7 %while.40 = (s32[]{:T(128)}, f32[3,312]{1,0:T(4,128)S(1)}, f32[3,3,416]{2,0,1:T(4,128)S(1)}, f32[1,3,312]{2,1,0:T(4,128)S(1)}, f32[3,3,416]{2,0,1:T(4,128)S(1)}, /*index=5*/s32[]{:T(128)}, s32[]{:T(128)}) while((s32[]{:T(128)}, f32[3,312]{1,0:T(4,128)S(1)}, f32[3,3,416]{2,0,1:T(4,128)S(1)}, f32[1,3,312]{2,1,0:T(4,128)S(1)}, ...), condition=%wide.region_5.5_spmd.clone, body=%wide.region_1.4_spmd.clone.sunk | while | flops 4154283 | bytes 4235803 | solution.py:38
  175.8 3.7 %while.41 = (s32[]{:T(128)}, f32[3,312]{1,0:T(4,128)S(1)}, f32[3,3,416]{2,0,1:T(4,128)S(1)}, f32[1,3,312]{2,1,0:T(4,128)S(1)}, f32[3,3,416]{2,0,1:T(4,128)S(1)}, /*index=5*/s32[]{:T(128)}, s32[]{:T(128)}) while((s32[]{:T(128)}, f32[3,312]{1,0:T(4,128)S(1)}, f32[3,3,416]{2,0,1:T(4,128)S(1)}, f32[1,3,312]{2,1,0:T(4,128)S(1)}, ...), condition=%wide.region_10.10_spmd.clone, body=%wide.region_6.9_spmd.clone.sunk | while | flops 4154283 | bytes 4235803 | solution.py:38
  180.9 3.7 %while.40 = (s32[]{:T(128)}, f32[3,312]{1,0:T(4,128)S(1)}, f32[3,3,416]{2,0,1:T(4,128)S(1)}, f32[1,3,312]{2,1,0:T(4,128)S(1)}, f32[3,3,416]{2,0,1:T(4,128)S(1)}, /*index=5*/s32[]{:T(128)}, s32[]{:T(128)}) while((s32[]{:T(128)}, f32[3,312]{1,0:T(4,128)S(1)}, f32[3,3,416]{2,0,1:T(4,128)S(1)}, f32[1,3,312]{2,1,0:T(4,128)S(1)}, ...), condition=%wide.region_5.5_spmd.clone, body=%wide.region_1.4_spmd.clone.sunk | while | flops 4154283 | bytes 4235803 | solution.py:38
  191.0 3.7 %while.41 = (s32[]{:T(128)}, f32[3,312]{1,0:T(4,128)S(1)}, f32[3,3,416]{2,0,1:T(4,128)S(1)}, f32[1,3,312]{2,1,0:T(4,128)S(1)}, f32[3,3,416]{2,0,1:T(4,128)S(1)}, /*index=5*/s32[]{:T(128)}, s32[]{:T(128)}) while((s32[]{:T(128)}, f32[3,312]{1,0:T(4,128)S(1)}, f32[3,3,416]{2,0,1:T(4,128)S(1)}, f32[1,3,312]{2,1,0:T(4,128)S(1)}, ...), condition=%wide.region_10.10_spmd.clone, body=%wide.region_6.9_spmd.clone.sunk | while | flops 4154283 | bytes 4235803 | solution.py:38
  196.1 3.7 %while.40 = (s32[]{:T(128)}, f32[3,312]{1,0:T(4,128)S(1)}, f32[3,3,416]{2,0,1:T(4,128)S(1)}, f32[1,3,312]{2,1,0:T(4,128)S(1)}, f32[3,3,416]{2,0,1:T(4,128)S(1)}, /*index=5*/s32[]{:T(128)}, s32[]{:T(128)}) while((s32[]{:T(128)}, f32[3,312]{1,0:T(4,128)S(1)}, f32[3,3,416]{2,0,1:T(4,128)S(1)}, f32[1,3,312]{2,1,0:T(4,128)S(1)}, ...), condition=%wide.region_5.5_spmd.clone, body=%wide.region_1.4_spmd.clone.sunk | while | flops 4154283 | bytes 4235803 | solution.py:38
  206.2 3.7 %while.41 = (s32[]{:T(128)}, f32[3,312]{1,0:T(4,128)S(1)}, f32[3,3,416]{2,0,1:T(4,128)S(1)}, f32[1,3,312]{2,1,0:T(4,128)S(1)}, f32[3,3,416]{2,0,1:T(4,128)S(1)}, /*index=5*/s32[]{:T(128)}, s32[]{:T(128)}) while((s32[]{:T(128)}, f32[3,312]{1,0:T(4,128)S(1)}, f32[3,3,416]{2,0,1:T(4,128)S(1)}, f32[1,3,312]{2,1,0:T(4,128)S(1)}, ...), condition=%wide.region_10.10_spmd.clone, body=%wide.region_6.9_spmd.clone.sunk | while | flops 4154283 | bytes 4235803 | solution.py:38
  211.2 3.7 %while.40 = (s32[]{:T(128)}, f32[3,312]{1,0:T(4,128)S(1)}, f32[3,3,416]{2,0,1:T(4,128)S(1)}, f32[1,3,312]{2,1,0:T(4,128)S(1)}, f32[3,3,416]{2,0,1:T(4,128)S(1)}, /*index=5*/s32[]{:T(128)}, s32[]{:T(128)}) while((s32[]{:T(128)}, f32[3,312]{1,0:T(4,128)S(1)}, f32[3,3,416]{2,0,1:T(4,128)S(1)}, f32[1,3,312]{2,1,0:T(4,128)S(1)}, ...), condition=%wide.region_5.5_spmd.clone, body=%wide.region_1.4_spmd.clone.sunk | while | flops 4154283 | bytes 4235803 | solution.py:38
  221.4 3.7 %while.41 = (s32[]{:T(128)}, f32[3,312]{1,0:T(4,128)S(1)}, f32[3,3,416]{2,0,1:T(4,128)S(1)}, f32[1,3,312]{2,1,0:T(4,128)S(1)}, f32[3,3,416]{2,0,1:T(4,128)S(1)}, /*index=5*/s32[]{:T(128)}, s32[]{:T(128)}) while((s32[]{:T(128)}, f32[3,312]{1,0:T(4,128)S(1)}, f32[3,3,416]{2,0,1:T(4,128)S(1)}, f32[1,3,312]{2,1,0:T(4,128)S(1)}, ...), condition=%wide.region_10.10_spmd.clone, body=%wide.region_6.9_spmd.clone.sunk | while | flops 4154283 | bytes 4235803 | solution.py:38
  226.4 3.7 %while.40 = (s32[]{:T(128)}, f32[3,312]{1,0:T(4,128)S(1)}, f32[3,3,416]{2,0,1:T(4,128)S(1)}, f32[1,3,312]{2,1,0:T(4,128)S(1)}, f32[3,3,416]{2,0,1:T(4,128)S(1)}, /*index=5*/s32[]{:T(128)}, s32[]{:T(128)}) while((s32[]{:T(128)}, f32[3,312]{1,0:T(4,128)S(1)}, f32[3,3,416]{2,0,1:T(4,128)S(1)}, f32[1,3,312]{2,1,0:T(4,128)S(1)}, ...), condition=%wide.region_5.5_spmd.clone, body=%wide.region_1.4_spmd.clone.sunk | while | flops 4154283 | bytes 4235803 | solution.py:38
  236.6 3.7 %while.41 = (s32[]{:T(128)}, f32[3,312]{1,0:T(4,128)S(1)}, f32[3,3,416]{2,0,1:T(4,128)S(1)}, f32[1,3,312]{2,1,0:T(4,128)S(1)}, f32[3,3,416]{2,0,1:T(4,128)S(1)}, /*index=5*/s32[]{:T(128)}, s32[]{:T(128)}) while((s32[]{:T(128)}, f32[3,312]{1,0:T(4,128)S(1)}, f32[3,3,416]{2,0,1:T(4,128)S(1)}, f32[1,3,312]{2,1,0:T(4,128)S(1)}, ...), condition=%wide.region_10.10_spmd.clone, body=%wide.region_6.9_spmd.clone.sunk | while | flops 4154283 | bytes 4235803 | solution.py:38
  241.6 3.7 %while.40 = (s32[]{:T(128)}, f32[3,312]{1,0:T(4,128)S(1)}, f32[3,3,416]{2,0,1:T(4,128)S(1)}, f32[1,3,312]{2,1,0:T(4,128)S(1)}, f32[3,3,416]{2,0,1:T(4,128)S(1)}, /*index=5*/s32[]{:T(128)}, s32[]{:T(128)}) while((s32[]{:T(128)}, f32[3,312]{1,0:T(4,128)S(1)}, f32[3,3,416]{2,0,1:T(4,128)S(1)}, f32[1,3,312]{2,1,0:T(4,128)S(1)}, ...), condition=%wide.region_5.5_spmd.clone, body=%wide.region_1.4_spmd.clone.sunk | while | flops 4154283 | bytes 4235803 | solution.py:38
  251.8 3.7 %while.41 = (s32[]{:T(128)}, f32[3,312]{1,0:T(4,128)S(1)}, f32[3,3,416]{2,0,1:T(4,128)S(1)}, f32[1,3,312]{2,1,0:T(4,128)S(1)}, f32[3,3,416]{2,0,1:T(4,128)S(1)}, /*index=5*/s32[]{:T(128)}, s32[]{:T(128)}) while((s32[]{:T(128)}, f32[3,312]{1,0:T(4,128)S(1)}, f32[3,3,416]{2,0,1:T(4,128)S(1)}, f32[1,3,312]{2,1,0:T(4,128)S(1)}, ...), condition=%wide.region_10.10_spmd.clone, body=%wide.region_6.9_spmd.clone.sunk | while | flops 4154283 | bytes 4235803 | solution.py:38
  256.8 3.7 %while.40 = (s32[]{:T(128)}, f32[3,312]{1,0:T(4,128)S(1)}, f32[3,3,416]{2,0,1:T(4,128)S(1)}, f32[1,3,312]{2,1,0:T(4,128)S(1)}, f32[3,3,416]{2,0,1:T(4,128)S(1)}, /*index=5*/s32[]{:T(128)}, s32[]{:T(128)}) while((s32[]{:T(128)}, f32[3,312]{1,0:T(4,128)S(1)}, f32[3,3,416]{2,0,1:T(4,128)S(1)}, f32[1,3,312]{2,1,0:T(4,128)S(1)}, ...), condition=%wide.region_5.5_spmd.clone, body=%wide.region_1.4_spmd.clone.sunk | while | flops 4154283 | bytes 4235803 | solution.py:38
  267.0 3.7 %while.41 = (s32[]{:T(128)}, f32[3,312]{1,0:T(4,128)S(1)}, f32[3,3,416]{2,0,1:T(4,128)S(1)}, f32[1,3,312]{2,1,0:T(4,128)S(1)}, f32[3,3,416]{2,0,1:T(4,128)S(1)}, /*index=5*/s32[]{:T(128)}, s32[]{:T(128)}) while((s32[]{:T(128)}, f32[3,312]{1,0:T(4,128)S(1)}, f32[3,3,416]{2,0,1:T(4,128)S(1)}, f32[1,3,312]{2,1,0:T(4,128)S(1)}, ...), condition=%wide.region_10.10_spmd.clone, body=%wide.region_6.9_spmd.clone.sunk | while | flops 4154283 | bytes 4235803 | solution.py:38
  272.0 3.7 %while.40 = (s32[]{:T(128)}, f32[3,312]{1,0:T(4,128)S(1)}, f32[3,3,416]{2,0,1:T(4,128)S(1)}, f32[1,3,312]{2,1,0:T(4,128)S(1)}, f32[3,3,416]{2,0,1:T(4,128)S(1)}, /*index=5*/s32[]{:T(128)}, s32[]{:T(128)}) while((s32[]{:T(128)}, f32[3,312]{1,0:T(4,128)S(1)}, f32[3,3,416]{2,0,1:T(4,128)S(1)}, f32[1,3,312]{2,1,0:T(4,128)S(1)}, ...), condition=%wide.region_5.5_spmd.clone, body=%wide.region_1.4_spmd.clone.sunk | while | flops 4154283 | bytes 4235803 | solution.py:38
  282.1 3.7 %while.41 = (s32[]{:T(128)}, f32[3,312]{1,0:T(4,128)S(1)}, f32[3,3,416]{2,0,1:T(4,128)S(1)}, f32[1,3,312]{2,1,0:T(4,128)S(1)}, f32[3,3,416]{2,0,1:T(4,128)S(1)}, /*index=5*/s32[]{:T(128)}, s32[]{:T(128)}) while((s32[]{:T(128)}, f32[3,312]{1,0:T(4,128)S(1)}, f32[3,3,416]{2,0,1:T(4,128)S(1)}, f32[1,3,312]{2,1,0:T(4,128)S(1)}, ...), condition=%wide.region_10.10_spmd.clone, body=%wide.region_6.9_spmd.clone.sunk | while | flops 4154283 | bytes 4235803 | solution.py:38
  287.2 3.7 %while.40 = (s32[]{:T(128)}, f32[3,312]{1,0:T(4,128)S(1)}, f32[3,3,416]{2,0,1:T(4,128)S(1)}, f32[1,3,312]{2,1,0:T(4,128)S(1)}, f32[3,3,416]{2,0,1:T(4,128)S(1)}, /*index=5*/s32[]{:T(128)}, s32[]{:T(128)}) while((s32[]{:T(128)}, f32[3,312]{1,0:T(4,128)S(1)}, f32[3,3,416]{2,0,1:T(4,128)S(1)}, f32[1,3,312]{2,1,0:T(4,128)S(1)}, ...), condition=%wide.region_5.5_spmd.clone, body=%wide.region_1.4_spmd.clone.sunk | while | flops 4154283 | bytes 4235803 | solution.py:38
  297.3 3.7 %while.41 = (s32[]{:T(128)}, f32[3,312]{1,0:T(4,128)S(1)}, f32[3,3,416]{2,0,1:T(4,128)S(1)}, f32[1,3,312]{2,1,0:T(4,128)S(1)}, f32[3,3,416]{2,0,1:T(4,128)S(1)}, /*index=5*/s32[]{:T(128)}, s32[]{:T(128)}) while((s32[]{:T(128)}, f32[3,312]{1,0:T(4,128)S(1)}, f32[3,3,416]{2,0,1:T(4,128)S(1)}, f32[1,3,312]{2,1,0:T(4,128)S(1)}, ...), condition=%wide.region_10.10_spmd.clone, body=%wide.region_6.9_spmd.clone.sunk | while | flops 4154283 | bytes 4235803 | solution.py:38
  302.4 3.7 %while.40 = (s32[]{:T(128)}, f32[3,312]{1,0:T(4,128)S(1)}, f32[3,3,416]{2,0,1:T(4,128)S(1)}, f32[1,3,312]{2,1,0:T(4,128)S(1)}, f32[3,3,416]{2,0,1:T(4,128)S(1)}, /*index=5*/s32[]{:T(128)}, s32[]{:T(128)}) while((s32[]{:T(128)}, f32[3,312]{1,0:T(4,128)S(1)}, f32[3,3,416]{2,0,1:T(4,128)S(1)}, f32[1,3,312]{2,1,0:T(4,128)S(1)}, ...), condition=%wide.region_5.5_spmd.clone, body=%wide.region_1.4_spmd.clone.sunk | while | flops 4154283 | bytes 4235803 | solution.py:38
  312.5 3.7 %while.41 = (s32[]{:T(128)}, f32[3,312]{1,0:T(4,128)S(1)}, f32[3,3,416]{2,0,1:T(4,128)S(1)}, f32[1,3,312]{2,1,0:T(4,128)S(1)}, f32[3,3,416]{2,0,1:T(4,128)S(1)}, /*index=5*/s32[]{:T(128)}, s32[]{:T(128)}) while((s32[]{:T(128)}, f32[3,312]{1,0:T(4,128)S(1)}, f32[3,3,416]{2,0,1:T(4,128)S(1)}, f32[1,3,312]{2,1,0:T(4,128)S(1)}, ...), condition=%wide.region_10.10_spmd.clone, body=%wide.region_6.9_spmd.clone.sunk | while | flops 4154283 | bytes 4235803 | solution.py:38
  317.6 3.7 %while.40 = (s32[]{:T(128)}, f32[3,312]{1,0:T(4,128)S(1)}, f32[3,3,416]{2,0,1:T(4,128)S(1)}, f32[1,3,312]{2,1,0:T(4,128)S(1)}, f32[3,3,416]{2,0,1:T(4,128)S(1)}, /*index=5*/s32[]{:T(128)}, s32[]{:T(128)}) while((s32[]{:T(128)}, f32[3,312]{1,0:T(4,128)S(1)}, f32[3,3,416]{2,0,1:T(4,128)S(1)}, f32[1,3,312]{2,1,0:T(4,128)S(1)}, ...), condition=%wide.region_5.5_spmd.clone, body=%wide.region_1.4_spmd.clone.sunk | while | flops 4154283 | bytes 4235803 | solution.py:38
  323.2 2.8 collective-permute-start.12
  328.3 4.1 %collective-permute-done.13 = f32[1,3,3,4,3,312]{5,3,2,1,0,4:T(4,128)S(1)} collective-permute-done((f32[1,3,3,4,3,312]{5,3,2,1,0,4:T(4,128)S(1)}, f32[1,3,3,4,3,312]{5,3,2,1,0,4:T(4,128)S(1)}, u32[]{:S(2)}, u32[]{:S(2)}) %collective-permute-start.13) | collective-permute-done | bytes 134816 | tf_op jit(solution)/shard_map/ppermute | solution.py:19
  332.5 2.9 collective-permute-start.14
  335.5 1.3 collective-permute-start.15
  336.8 2.4 collective-permute-done.14
  339.2 4.1 %collective-permute-done.15 = f32[5,1,3,4,3,312]{5,3,2,1,0,4:T(4,128)S(1)} collective-permute-done((f32[5,1,3,4,3,312]{5,3,2,1,0,4:T(4,128)S(1)}, f32[5,1,3,4,3,312]{5,3,2,1,0,4:T(4,128)S(1)}, u32[]{:S(2)}, u32[]{:S(2)}) %collective-permute-start.15) | collective-permute-done | bytes 224672 | tf_op jit(solution)/shard_map/ppermute | solution.py:19
  343.6 3.9 %collective-permute-start.16 = (f32[5,5,1,4,3,312]{5,3,2,1,0,4:T(4,128)S(1)}, f32[5,5,1,4,3,312]{5,3,2,1,0,4:T(4,128)S(1)}, u32[]{:S(2)}, u32[]{:S(2)}) collective-permute-start(f32[5,5,1,4,3,312]{5,3,2,1,0,4:T(4,128)S(1)} %get-tuple-element.280), channel_id=1, source_target_pairs={{0,1},{1,2},{2,3},{3,4},{4,5},{5,6},{6,7},{7,8},{8,9},{9,10},{10,1... | collective-permute-start | bytes 1123208 | tf_op jit(solution)/shard_map/ppermute | solution.py:16
  347.5 2.1 collective-permute-start.17
  349.5 3.4 collective-permute-done.16
  352.9 5.7 %collective-permute-done.17 = f32[5,5,1,4,3,312]{5,3,2,1,0,4:T(4,128)S(1)} collective-permute-done((f32[5,5,1,4,3,312]{5,3,2,1,0,4:T(4,128)S(1)}, f32[5,5,1,4,3,312]{5,3,2,1,0,4:T(4,128)S(1)}, u32[]{:S(2)}, u32[]{:S(2)}) %collective-permute-start.17) | collective-permute-done | bytes 374432 | tf_op jit(solution)/shard_map/ppermute | solution.py:19
  (1037 shorter events, 180.5 us)
Async XLA Ops:
  0.0 1.4 copy-start
  0.0 4.4 %copy-start.2 = (f32[312,169]{0,1:T(8,128)S(1)}, f32[312,169]{0,1:T(8,128)}, u32[]{:S(2)}) copy-start(f32[312,169]{0,1:T(8,128)} %param.15) | copy-start | bytes 632740
  5.7 32.9 %copy-start.1 = (f32[1,1,1,4,3,312]{5,3,4,2,1,0:T(4,128)S(1)}, f32[1,1,1,4,3,312]{5,3,4,2,1,0:T(4,128)}, u32[]{:S(2)}) copy-start(f32[1,1,1,4,3,312]{5,3,4,2,1,0:T(4,128)} %param.14) | copy-start | bytes 44932
  5.7 45.4 %copy-start.9 = (s32[1,1,1,16,3]{3,2,4,1,0:T(1,128)S(1)}, s32[1,1,1,16,3]{3,2,4,1,0:T(1,128)}, u32[]{:S(2)}) copy-start(s32[1,1,1,16,3]{3,2,4,1,0:T(1,128)} %param.20) | copy-start | bytes 580
  5.7 58.9 %copy-start.7 = (f32[1248]{0:T(1024)S(1)}, f32[1248]{0:T(1024)}, u32[]{:S(2)}) copy-start(f32[1248]{0:T(1024)} %param.19) | copy-start | bytes 14980
  5.7 5.0 %collective-permute-start = (f32[1,1,1,4,2,3,1248]{6,3,5,4,2,1,0:T(4,128)S(1)}, f32[1,1,1,4,2,3,1248]{6,3,5,4,2,1,0:T(4,128)S(1)}, u32[]{:S(2)}, u32[]{:S(2)}) collective-permute-start(f32[1,1,1,4,2,3,1248]{6,3,5,4,2,1,0:T(4,128)S(1)} %maximum_bitcast_fusion), channel_id=1, source_target_pairs={{0,64},{64,128},{128,192},{1,65},{65,129},{129,193},{2,66},{66,130... | collective-permute-start | bytes 359432 | tf_op jit(solution)/shard_map/ppermute | solution.py:16
  8.9 5.6 %collective-permute-start.1 = (f32[1,1,1,4,2,3,1248]{6,3,5,4,2,1,0:T(4,128)S(1)}, f32[1,1,1,4,2,3,1248]{6,3,5,4,2,1,0:T(4,128)S(1)}, u32[]{:S(2)}, u32[]{:S(2)}) collective-permute-start(f32[1,1,1,4,2,3,1248]{6,3,5,4,2,1,0:T(4,128)S(1)} %maximum_bitcast_fusion), channel_id=1, source_target_pairs={{64,0},{128,64},{192,128},{65,1},{129,65},{193,129},{66,2},{130,66... | collective-permute-start | bytes 359432 | tf_op jit(solution)/shard_map/ppermute | solution.py:19
  14.6 9.0 %collective-permute-start.2 = (f32[3,1,1,4,2,3,1248]{6,3,5,4,2,1,0:T(4,128)S(1)}, f32[3,1,1,4,2,3,1248]{6,3,5,4,2,1,0:T(4,128)S(1)}, u32[]{:S(2)}, u32[]{:S(2)}) collective-permute-start(f32[3,1,1,4,2,3,1248]{6,3,5,4,2,1,0:T(4,128)S(1)} %pad_maximum_fusion.9), channel_id=1, source_target_pairs={{0,16},{16,32},{32,48},{1,17},{17,33},{33,49},{2,18},{18,34},{34,5... | collective-permute-start | bytes 1078280 | tf_op jit(solution)/shard_map/ppermute | solution.py:16
  17.8 9.6 %collective-permute-start.3 = (f32[3,1,1,4,2,3,1248]{6,3,5,4,2,1,0:T(4,128)S(1)}, f32[3,1,1,4,2,3,1248]{6,3,5,4,2,1,0:T(4,128)S(1)}, u32[]{:S(2)}, u32[]{:S(2)}) collective-permute-start(f32[3,1,1,4,2,3,1248]{6,3,5,4,2,1,0:T(4,128)S(1)} %pad_maximum_fusion.9), channel_id=1, source_target_pairs={{16,0},{32,16},{48,32},{17,1},{33,17},{49,33},{18,2},{34,18},{50,3... | collective-permute-start | bytes 1078280 | tf_op jit(solution)/shard_map/ppermute | solution.py:19
  28.7 42.6 %collective-permute-start.4 = (f32[3,3,1,4,2,3,1248]{6,3,5,4,2,1,0:T(4,128)}, f32[3,3,1,4,2,3,1248]{6,3,5,4,2,1,0:T(4,128)}, u32[]{:S(2)}, u32[]{:S(2)}) collective-permute-start(f32[3,3,1,4,2,3,1248]{6,3,5,4,2,1,0:T(4,128)} %pad_maximum_fusion.2), channel_id=1, source_target_pairs={{0,1},{1,2},{2,3},{3,4},{4,5},{5,6},{6,7},{7,8},{8,9},{9,10},{10,1... | collective-permute-start | bytes 3234824 | tf_op jit(solution)/shard_map/ppermute | solution.py:16
  36.6 34.7 %collective-permute-start.5 = (f32[3,3,1,4,2,3,1248]{6,3,5,4,2,1,0:T(4,128)}, f32[3,3,1,4,2,3,1248]{6,3,5,4,2,1,0:T(4,128)}, u32[]{:S(2)}, u32[]{:S(2)}) collective-permute-start(f32[3,3,1,4,2,3,1248]{6,3,5,4,2,1,0:T(4,128)} %pad_maximum_fusion.2), channel_id=1, source_target_pairs={{1,0},{2,1},{3,2},{4,3},{5,4},{6,5},{7,6},{8,7},{9,8},{10,9},{11,1... | collective-permute-start | bytes 3234824 | tf_op jit(solution)/shard_map/ppermute | solution.py:19
  38.6 4.4 %collective-permute-start.6 = (f32[1,1,1,4,3,312]{5,3,4,2,1,0:T(4,128)S(1)}, f32[1,1,1,4,3,312]{5,3,4,2,1,0:T(4,128)S(1)}, u32[]{:S(2)}, u32[]{:S(2)}) collective-permute-start(f32[1,1,1,4,3,312]{5,3,4,2,1,0:T(4,128)S(1)} %copy-done.1), channel_id=1, source_target_pairs={{0,64},{64,128},{128,192},{1,65},{65,129},{129,193},{2,66},{66,130... | collective-permute-start | bytes 44936 | tf_op jit(solution)/shard_map/ppermute | solution.py:16
  41.7 4.9 %collective-permute-start.7 = (f32[1,1,1,4,3,312]{5,3,4,2,1,0:T(4,128)S(1)}, f32[1,1,1,4,3,312]{5,3,4,2,1,0:T(4,128)S(1)}, u32[]{:S(2)}, u32[]{:S(2)}) collective-permute-start(f32[1,1,1,4,3,312]{5,3,4,2,1,0:T(4,128)S(1)} %copy-done.1), channel_id=1, source_target_pairs={{64,0},{128,64},{192,128},{65,1},{129,65},{193,129},{66,2},{130,66... | collective-permute-start | bytes 44936 | tf_op jit(solution)/shard_map/ppermute | solution.py:19
  46.6 4.5 %collective-permute-start.8 = (f32[3,1,1,4,3,312]{5,3,4,2,1,0:T(4,128)S(1)}, f32[3,1,1,4,3,312]{5,3,4,2,1,0:T(4,128)S(1)}, u32[]{:S(2)}, u32[]{:S(2)}) collective-permute-start(f32[3,1,1,4,3,312]{5,3,4,2,1,0:T(4,128)S(1)} %constant_dynamic-update-slice_fusion), channel_id=1, source_target_pairs={{0,16},{16,32},{32,48},{1,17},{17,33},{33,49},{2,18},{18,34},{34,5... | collective-permute-start | bytes 134792 | tf_op jit(solution)/shard_map/ppermute | solution.py:16
  49.8 4.9 %collective-permute-start.9 = (f32[3,1,1,4,3,312]{5,3,4,2,1,0:T(4,128)S(1)}, f32[3,1,1,4,3,312]{5,3,4,2,1,0:T(4,128)S(1)}, u32[]{:S(2)}, u32[]{:S(2)}) collective-permute-start(f32[3,1,1,4,3,312]{5,3,4,2,1,0:T(4,128)S(1)} %constant_dynamic-update-slice_fusion), channel_id=1, source_target_pairs={{16,0},{32,16},{48,32},{17,1},{33,17},{49,33},{18,2},{34,18},{50,3... | collective-permute-start | bytes 134792 | tf_op jit(solution)/shard_map/ppermute | solution.py:19
  54.7 10.6 %collective-permute-start.10 = (f32[3,3,1,4,3,312]{5,3,4,2,1,0:T(4,128)S(1)}, f32[3,3,1,4,3,312]{5,3,4,2,1,0:T(4,128)}, u32[]{:S(2)}, u32[]{:S(2)}) collective-permute-start(f32[3,3,1,4,3,312]{5,3,4,2,1,0:T(4,128)S(1)} %pad_maximum_fusion.13), channel_id=1, source_target_pairs={{0,1},{1,2},{2,3},{3,4},{4,5},{5,6},{6,7},{7,8},{8,9},{9,10},{10,1... | collective-permute-start | bytes 404360 | tf_op jit(solution)/shard_map/ppermute | solution.py:16
  62.0 8.0 %collective-permute-start.11 = (f32[3,3,1,4,3,312]{5,3,4,2,1,0:T(4,128)S(1)}, f32[3,3,1,4,3,312]{5,3,4,2,1,0:T(4,128)}, u32[]{:S(2)}, u32[]{:S(2)}) collective-permute-start(f32[3,3,1,4,3,312]{5,3,4,2,1,0:T(4,128)S(1)} %pad_maximum_fusion.13), channel_id=1, source_target_pairs={{1,0},{2,1},{3,2},{4,3},{5,4},{6,5},{7,6},{8,7},{9,8},{10,9},{11,1... | collective-permute-start | bytes 404360 | tf_op jit(solution)/shard_map/ppermute | solution.py:19
  75.1 3.2 copy-start.3
  75.1 3.2 copy-start.4
  75.1 3.2 copy-start.8
  321.4 0.6 copy-start.5
  323.2 5.1 %collective-permute-start.12 = (f32[1,3,3,4,3,312]{5,3,2,1,4,0:T(4,128)S(1)}, f32[1,3,3,4,3,312]{5,3,2,1,4,0:T(4,128)S(1)}, u32[]{:S(2)}, u32[]{:S(2)}) collective-permute-start(f32[1,3,3,4,3,312]{5,3,2,1,4,0:T(4,128)S(1)} %slice.40), channel_id=1, source_target_pairs={{0,64},{64,128},{128,192},{1,65},{65,129},{129,193},{2,66},{66,130... | collective-permute-start | bytes 404360 | tf_op jit(solution)/shard_map/ppermute | solution.py:16
  326.3 6.1 %collective-permute-start.13 = (f32[1,3,3,4,3,312]{5,3,2,1,0,4:T(4,128)S(1)}, f32[1,3,3,4,3,312]{5,3,2,1,0,4:T(4,128)S(1)}, u32[]{:S(2)}, u32[]{:S(2)}) collective-permute-start(f32[1,3,3,4,3,312]{5,3,2,1,0,4:T(4,128)S(1)} %bitcast.139), channel_id=1, source_target_pairs={{64,0},{128,64},{192,128},{65,1},{129,65},{193,129},{66,2},{130,66... | collective-permute-start | bytes 404360 | tf_op jit(solution)/shard_map/ppermute | solution.py:19
  332.5 6.7 %collective-permute-start.14 = (f32[5,1,3,4,3,312]{5,3,2,1,0,4:T(4,128)S(1)}, f32[5,1,3,4,3,312]{5,3,2,1,0,4:T(4,128)S(1)}, u32[]{:S(2)}, u32[]{:S(2)}) collective-permute-start(f32[5,1,3,4,3,312]{5,3,2,1,0,4:T(4,128)S(1)} %get-tuple-element.282), channel_id=1, source_target_pairs={{0,16},{16,32},{32,48},{1,17},{17,33},{33,49},{2,18},{18,34},{34,5... | collective-permute-start | bytes 673928 | tf_op jit(solution)/shard_map/ppermute | solution.py:16
  335.5 7.9 %collective-permute-start.15 = (f32[5,1,3,4,3,312]{5,3,2,1,0,4:T(4,128)S(1)}, f32[5,1,3,4,3,312]{5,3,2,1,0,4:T(4,128)S(1)}, u32[]{:S(2)}, u32[]{:S(2)}) collective-permute-start(f32[5,1,3,4,3,312]{5,3,2,1,0,4:T(4,128)S(1)} %get-tuple-element.283), channel_id=1, source_target_pairs={{16,0},{32,16},{48,32},{17,1},{33,17},{49,33},{18,2},{34,18},{50,3... | collective-permute-start | bytes 673928 | tf_op jit(solution)/shard_map/ppermute | solution.py:19
  343.6 9.3 %collective-permute-start.16 = (f32[5,5,1,4,3,312]{5,3,2,1,0,4:T(4,128)S(1)}, f32[5,5,1,4,3,312]{5,3,2,1,0,4:T(4,128)S(1)}, u32[]{:S(2)}, u32[]{:S(2)}) collective-permute-start(f32[5,5,1,4,3,312]{5,3,2,1,0,4:T(4,128)S(1)} %get-tuple-element.280), channel_id=1, source_target_pairs={{0,1},{1,2},{2,3},{3,4},{4,5},{5,6},{6,7},{7,8},{8,9},{9,10},{10,1... | collective-permute-start | bytes 1123208 | tf_op jit(solution)/shard_map/ppermute | solution.py:16
  347.5 11.8 %copy-start.6 = (f32[16,3,312]{2,0,1:T(8,128)S(1)}, f32[16,3,312]{2,0,1:T(8,128)}, u32[]{:S(2)}) copy-start(f32[16,3,312]{2,0,1:T(8,128)} %copy-done.5) | copy-start | bytes 179716
  347.5 11.2 %collective-permute-start.17 = (f32[5,5,1,4,3,312]{5,3,2,1,0,4:T(4,128)S(1)}, f32[5,5,1,4,3,312]{5,3,2,1,0,4:T(4,128)S(1)}, u32[]{:S(2)}, u32[]{:S(2)}) collective-permute-start(f32[5,5,1,4,3,312]{5,3,2,1,0,4:T(4,128)S(1)} %get-tuple-element.281), channel_id=1, source_target_pairs={{1,0},{2,1},{3,2},{4,3},{5,4},{6,5},{7,6},{8,7},{9,8},{10,9},{11,1... | collective-permute-start | bytes 1123208 | tf_op jit(solution)/shard_map/ppermute | solution.py:19
where the time goes:
time: 363 us; the launch traced here: 360 us
  other arithmetic  117 us (32%)
  loops' own time  77.4 us (21%)
  local copies, waits for them, and re-layouts  63.3 us (17%)
  starting transfers between devices  51.2 us (14%)
  waiting for transfers between devices  44.5 us (12%)
  matrix products  5.59 us (2%)
    another operation x1, loops' own time, shards(): on_near, on_far = lax.map(per_pair, (own_slot, far_rows, slot_used))  71.9 us
    reduce_sum x96, other arithmetic, add_block(): return (running + jnp.sum(summand, axis=2), None)  55.9 us
    ppermute x9, starting transfers between devices, with_halo(): lax.ppermute(lax.slice_in_dim(block, block.shape[dim] - width, None, axis...  37.6 us
    reduce_sum x96, other arithmetic, add_block(): inverse = 1.0 / jnp.sqrt(jnp.sum(offset * offset, axis=0) + smooth_sq)  37 us
    ppermute x9, waiting for transfers between devices, with_halo(): lax.ppermute(lax.slice_in_dim(block, 0, width, axis=dim), axis, backward)  33.4 us
    dynamic_slice x48, local copies, waits for them, and re-layouts, shards(): on_near, on_far = lax.map(per_pair, (own_slot, far_rows, slot_used))  30.3 us
    sqrt x96, other arithmetic, add_block(): inverse = 1.0 / jnp.sqrt(jnp.sum(offset * offset, axis=0) + smooth_sq)  16.2 us
    ppermute x9, starting transfers between devices, with_halo(): lax.ppermute(lax.slice_in_dim(block, 0, width, axis=dim), axis, backward)  13.6 us
  transfers between devices with their start and end apart: 18, of which 13 were waited for; matrix products, arithmetic and copies ran while one was open for 1% of the time, Pallas kernels for 0%

commit v1 on v0

v1 whole, which is shorter than its diff:
```python
import functools
import math

import jax
import jax.numpy as jnp
from jax import lax
from jax.experimental import pallas as pl
from jax.experimental.pallas import tpu as pltpu
from jax.sharding import PartitionSpec as P

MESH = pl.DeviceIdType.MESH
F32 = jnp.float32
BF16 = jnp.bfloat16
smooth_sq = 0.25

CELLS = 4
POINTS = 312
RAISED = 1248
SLOTS = 16
LANES = 128
PW = 384
RW = 1280
OWN = 13
LIST = 512
GROUP = 32
DEPTH = 80


def split2(x):
    high = x.astype(BF16)
    return high, (x - high.astype(F32)).astype(BF16)


def split3(x):
    a = x.astype(BF16).astype(F32)
    rest = x - a
    b = rest.astype(BF16).astype(F32)
    return a, b, rest - b


def dot_nt(a, b, precision=None):
    return lax.dot_general(
        a, b, (((1,), (1,)), ((), ())), preferred_element_type=F32, precision=precision
    )


def dot_nt3(a, b_high, b_low):
    high, low = split2(a)
    return dot_nt(high, b_high) + dot_nt(low, b_high) + dot_nt(high, b_low)


def exchange_kernel(
    surface, pairs, count, synthesis, analysis, stiffness, upsample,
    halo, table, target, own_bend, bend_high, bend_low, up_high, up_low,
    code_s, near_s, far_s, rows_s, own_s, send_sem, recv_sem,
):
    sizes = [lax.axis_size(a) for a in ("tx", "ty", "tz")]
    here = [lax.axis_index(a) for a in ("tx", "ty", "tz")]
    others = [n for n in range(27) if n != OWN]

    def at(n):
        step = (n // 9 - 1, n // 3 % 3 - 1, n % 3 - 1)
        return tuple(lax.rem(h + d + s, s) for h, d, s in zip(here, step, sizes))

    barrier = pltpu.get_barrier_semaphore()
    for n in others:
        pl.semaphore_signal(barrier, inc=1, device_id=at(n), device_id_type=MESH)

    own_s[...] = jnp.zeros((16, PW), F32)
    for c in range(CELLS):
        own_s[4 * c : 4 * c + 3, :POINTS] = surface[c]
    used = count[0]
    slot_row = lax.broadcasted_iota(jnp.int32, (SLOTS, LANES), 0)
    slot_lane = lax.broadcasted_iota(jnp.int32, (SLOTS, LANES), 1)
    columns = pairs[...].astype(F32)
    lane = lax.broadcasted_iota(jnp.int32, (1, LANES), 1)
    for k in range(3):
        column = jnp.broadcast_to(columns[:, k : k + 1], (SLOTS, LANES))
        row = jnp.sum(jnp.where(slot_row == slot_lane, column, 0.0), axis=0, keepdims=True)
        if k == 1:
            row = jnp.where(lane < used, row, -1.0)
        own_s[4 * k + 3 : 4 * k + 4, :LANES] = row
    for c in range(CELLS):
        halo[OWN, c] = own_s[4 * c : 4 * c + 4, :]

    pl.semaphore_wait(barrier, 26)

    copies = []
    for n in others:
        copy = pltpu.make_async_remote_copy(
            src_ref=halo.at[OWN],
            dst_ref=halo.at[26 - n],
            send_sem=send_sem.at[n],
            recv_sem=recv_sem.at[26 - n],
            device_id=at(n),
            device_id_type=MESH,
        )
        copy.start()
        copies.append(copy)

    highest = lax.Precision.HIGHEST
    bend = jnp.dot(
        synthesis[...] * stiffness[...], analysis[...],
        preferred_element_type=F32, precision=highest,
    )
    bend_high[...], bend_low[...] = split2(bend)
    own = own_s[...]
    own_bend[...] = dot_nt(own[:, :POINTS], bend, highest)
    raised = upsample[...]
    up_high[:RAISED, :], up_low[:RAISED, :] = split2(raised)
    up_high[RAISED:, :] = jnp.zeros((RW - RAISED, POINTS), BF16)
    up_low[RAISED:, :] = jnp.zeros((RW - RAISED, POINTS), BF16)
    ones = jnp.ones((3, PW), F32)
    for c in range(CELLS):
        t = own[4 * c : 4 * c + 3, :]
        norm = jnp.sum(t * t, axis=0, keepdims=True) + smooth_sq
        t1, t2, t3 = split3(t)
        s1, s2, s3 = split3(norm)
        for kind in range(2):
            at_row = 4 * kind
            scale = 1.0 if kind else -2.0
            rows_s[...] = jnp.zeros((LANES, PW), F32)
            for block, part in enumerate((t1, t1, t2, t2, t1, t3)):
                rows_s[8 * block + at_row : 8 * block + at_row + 3, :] = part * scale
            for block in (6, 7, 8):
                rows_s[8 * block + at_row : 8 * block + at_row + 3, :] = -ones if kind else ones
            if not kind:
                rows_s[72:73, :] = s1
                rows_s[73:74, :] = s2
                rows_s[74:75, :] = s3
            target[c, kind] = jnp.transpose(rows_s[...])[:POINTS].astype(BF16)

    for copy in copies:
        copy.wait_recv()

    for ref, k in ((near_s, 0), (code_s, 1), (far_s, 2)):
        ref[...] = jnp.full((LANES, LANES), -1.0, F32)
        for n in range(27):
            ref[n : n + 1, :] = halo[n, k, 3:4, :LANES]
        ref[27:28, :] = halo[OWN, k, 3:4, :LANES]
    place = lax.broadcasted_iota(jnp.int32, (32, LANES), 0)
    place_f = place.astype(F32)
    lane32 = lax.broadcasted_iota(jnp.int32, (32, LANES), 1)
    code, near, far = code_s[:32, :], near_s[:32, :], far_s[:32, :]
    mask = jnp.logical_or(
        jnp.logical_and(place < 27, code == 26.0 - place_f),
        jnp.logical_and(place == 27, code >= 0.0),
    )
    mask = jnp.logical_and(mask, lane32 < SLOTS)
    value = jnp.where(
        place == 27, near * 128.0 + (code * 4.0 + far), far * 128.0 + (place_f * 4.0 + near)
    )
    taken = mask.astype(F32)
    upper = (
        lax.broadcasted_iota(jnp.int32, (LANES, LANES), 0)
        < lax.broadcasted_iota(jnp.int32, (LANES, LANES), 1)
    ).astype(F32)
    lower = (
        lax.broadcasted_iota(jnp.int32, (32, 32), 1) < lax.broadcasted_iota(jnp.int32, (32, 32), 0)
    ).astype(F32)
    per_row = jnp.broadcast_to(jnp.sum(taken, axis=1, keepdims=True), (32, LANES))
    before = jnp.dot(taken, upper, preferred_element_type=F32)
    above = jnp.dot(lower, per_row, preferred_element_type=F32)
    code_s[:32, :] = jnp.where(mask, before + above, -1.0)
    near_s[:32, :] = value
    spot = jnp.transpose(code_s[...])[:SLOTS]
    value = jnp.transpose(near_s[...])[:SLOTS]
    index = lax.broadcasted_iota(jnp.int32, (SLOTS, LIST), 1).astype(F32)
    listed = jnp.zeros((SLOTS, LIST), F32)
    for n in range(28):
        listed = listed + jnp.where(spot[:, n : n + 1] == index, value[:, n : n + 1], 0.0)
    table[0:1, :] = jnp.sum(listed, axis=0, keepdims=True).astype(jnp.int32)
    total = jnp.sum(jnp.sum(taken, axis=1, keepdims=True), axis=0, keepdims=True)
    table[1:2, :] = jnp.broadcast_to(total, (1, LIST)).astype(jnp.int32)

    for copy in copies:
        copy.wait_send()


def sums_kernel(
    table, halo, target, own_bend, bend_high, bend_low, up_high, up_low, weight,
    velocity,
    source_s, raised_s, wide_s, square_s, along_s, total_s,
):
    count = table[1, 0]
    total_s[...] = jnp.zeros(total_s.shape, F32)
    row8 = lax.broadcasted_iota(jnp.int32, (8, RW), 0)

    def group(g, carry):
        first = g * GROUP
        last = jnp.minimum(first + GROUP, count)

        def pick(e, carry):
            cell = table[0, jnp.minimum(first + e, count - 1)] % 128
            rows = halo[cell // 4, cell % 4]
            source_s[e, 0:4, :] = rows
            source_s[e, 4:8, :] = rows
            return carry

        lax.fori_loop(0, GROUP, pick, 0)
        picked = source_s[...].reshape(GROUP * 8, PW)[:, :POINTS]
        bent = dot_nt3(picked, bend_high[...], bend_low[...])
        is_pos = lax.broadcasted_iota(jnp.int32, (GROUP * 8, POINTS), 0) % 8 < 4
        carried = jnp.where(is_pos, picked, bent)
        raised = dot_nt3(carried, up_high[...], up_low[...])
        raised_s[...] = raised.reshape(GROUP, 8, RW)

        def one(e, carry):
            item = table[0, first + e]
            cell = item // 128
            scale = jnp.where(row8 < 4, 1.0, weight[...])
            both = raised_s[e] * scale
            for c in range(3):
                wide_s[c] = jnp.broadcast_to(both[c : c + 1, :], (8, RW))
                wide_s[3 + c] = jnp.broadcast_to(both[4 + c : 5 + c, :], (8, RW))
            p1, p2, p3 = split3(both)
            m1, m2, m3 = split3(both * jnp.where(row8 < 4, both, pltpu.roll(both, 4, 0)))
            operand = jnp.concatenate(
                [p1, p2, p1, p2, p3, p1, m1, m2, m3, jnp.ones((8, RW), F32)], axis=0
            ).astype(BF16)
            square_s[...] = jnp.dot(target[cell, 0, :, :DEPTH], operand, preferred_element_type=F32)
            along_s[...] = jnp.dot(target[cell, 1, :, :DEPTH], operand, preferred_element_type=F32)

            def block(i, carry):
                at = pl.ds(pl.multiple_of(i * 8, 8), 8)
                inverse = lax.rsqrt(square_s[at, :])
                factor = along_s[at, :] * inverse * (inverse * inverse)

                def fold(x):
                    out = x[:, :LANES]
                    for k in range(1, RW // LANES):
                        out = out + x[:, k * LANES : (k + 1) * LANES]
                    return out

                total_s[cell, 3, at, :] += fold(factor)
                for c in range(3):
                    total_s[cell, c, at, :] += fold(wide_s[3 + c] * inverse - wide_s[c] * factor)
                return carry

            lax.fori_loop(0, POINTS // 8, block, 0)
            return carry

        lax.fori_loop(0, last - first, one, 0)
        return carry

    lax.fori_loop(0, (count + GROUP - 1) // GROUP, group, 0)

    ones = jnp.ones((8, LANES), BF16)

    def reduced(x):
        high, low = split2(x)
        return (dot_nt(ones, high) + dot_nt(ones, low))[0:1, :]

    for c in range(CELLS):
        weight_sum = reduced(total_s[c, 3])
        for k in range(3):
            row = 4 * c + k
            place = halo[OWN, c, k : k + 1, :POINTS]
            velocity[c, k : k + 1, :] = (
                0.25 * own_bend[row : row + 1, :]
                + reduced(total_s[c, k])
                + place * weight_sum
            )


VMEM = pl.BlockSpec(memory_space=pltpu.VMEM)
SMEM = pl.BlockSpec(memory_space=pltpu.SMEM)


def sums(table, halo, target, own_bend, bend_high, bend_low, up_high, up_low, weight):
    return pl.pallas_call(
        sums_kernel,
        out_shape=jax.ShapeDtypeStruct((CELLS, 3, POINTS), F32),
        in_specs=[SMEM] + [VMEM] * 8,
        out_specs=VMEM,
        scratch_shapes=[
            pltpu.VMEM((GROUP, 8, PW), F32),
            pltpu.VMEM((GROUP, 8, RW), F32),
            pltpu.VMEM((6, 8, RW), F32),
            pltpu.VMEM((POINTS, RW), F32),
            pltpu.VMEM((POINTS, RW), F32),
            pltpu.VMEM((CELLS, 4, POINTS, LANES), F32),
        ],
        compiler_params=pltpu.CompilerParams(vmem_limit_bytes=40 * 2**20),
        name="sums",
    )(table, halo, target, own_bend, bend_high, bend_low, up_high, up_low, weight)


def shards(surface, synthesis, analysis, stiffness, upsample, quad_weight, near_pairs, pair_count):
    outs = pl.pallas_call(
        exchange_kernel,
        out_shape=(
            jax.ShapeDtypeStruct((27, CELLS, 4, PW), F32),
            jax.ShapeDtypeStruct((2, LIST), jnp.int32),
            jax.ShapeDtypeStruct((CELLS, 2, POINTS, LANES), BF16),
            jax.ShapeDtypeStruct((16, POINTS), F32),
            jax.ShapeDtypeStruct((POINTS, POINTS), BF16),
            jax.ShapeDtypeStruct((POINTS, POINTS), BF16),
            jax.ShapeDtypeStruct((RW, POINTS), BF16),
            jax.ShapeDtypeStruct((RW, POINTS), BF16),
        ),
        in_specs=[VMEM, VMEM, SMEM] + [VMEM] * 4,
        out_specs=[VMEM] * 8,
        scratch_shapes=[
            pltpu.VMEM((LANES, LANES), F32),
            pltpu.VMEM((LANES, LANES), F32),
            pltpu.VMEM((LANES, LANES), F32),
            pltpu.VMEM((LANES, PW), F32),
            pltpu.VMEM((16, PW), F32),
            pltpu.SemaphoreType.DMA((27,)),
            pltpu.SemaphoreType.DMA((27,)),
        ],
        compiler_params=pltpu.CompilerParams(
            collective_id=0, has_side_effects=True, vmem_limit_bytes=40 * 2**20
        ),
        name="exchange",
    )(
        surface[0, 0, 0], near_pairs[0, 0, 0], pair_count.reshape(1),
        synthesis, analysis, stiffness[None, :], upsample,
    )
    halo, table, *prepared = outs
    weight = jnp.pad(quad_weight * (1.0 / math.sqrt(RAISED)), (0, RW - RAISED))[None, :]
    velocity = sums(table, halo, *prepared, weight)
    return velocity[None, None, None]


def solution(mesh):
    return jax.shard_map(
        shards,
        mesh=mesh,
        in_specs=(
            P("tx", "ty", "tz", None, None, None),
            P(),
            P(),
            P(),
            P(),
            P(),
            P("tx", "ty", "tz", None, None),
            P("tx", "ty", "tz"),
        ),
        out_specs=P("tx", "ty", "tz", None, None, None),
        check_vma=False,
    )
```

time: 363 us -> 78.4 us (0.22)
  the two profiles are of different devices: /device:TPU:97 before, /device:TPU:33 now
where the time goes in v1:
time: 78.4 us; the launch traced here: 78.2 us
  Pallas kernels  74.4 us (95%)
  local copies, waits for them, and re-layouts  3.05 us (4%)
    pallas_call x1, Pallas kernels, sums(): pl.pallas_call(sums_kernel, out_shape=jax.ShapeDtypeStruct((CELLS, 3, POI...  60.3 us
    pallas_call x1, Pallas kernels, shards(): pl.pallas_call(exchange_kernel, out_shape=(jax.ShapeDtypeStruct((27, CELL...  14.1 us
    unnamed x15, local copies, waits for them, and re-layouts  2.32 us

profile of v1, /device:TPU:33, one launch (start us, length us, event | category | flops | bytes accessed | tf_op | source)
XLA Modules:
  0.0 78.2 jit_solution(2107674518390090694)
XLA Ops:
  0.0 0.0 copy-start.2
  0.0 0.0 copy-start.3
  0.0 0.0 copy-start.5
  0.0 0.0 copy-start.1
  0.0 0.0 copy-start
  0.0 2.1 %copy.12.upsample = f32[1248,312]{1,0:T(8,128)S(1)} copy(f32[1248,312]{0,1:T(8,128)} %param.12) | data formatting | bytes 3115008 | tf_op args[4]
  2.2 0.0 copy-done.2
  2.2 0.0 copy-start.4
  2.2 0.1 copy.11.synthesis
  2.4 0.0 copy-done.3
  2.4 0.0 copy-done.5
  2.4 0.1 copy.14
  3.1 0.0 copy-done.1
  3.1 0.0 copy-done
  3.1 14.1 %exchange.1 = (f32[27,4,4,384]{3,2,1,0:T(4,128)S(1)}, s32[2,512]{1,0:T(2,128)S(1)}, bf16[4,2,312,128]{3,2,1,0:T(8,128)(2,1)S(1)}, f32[16,312]{1,0:T(8,128)S(1)},...) custom-call(f32[4,3,312]{2,1,0:T(4,128)S(1)} %bitcast.8, ...), custom_call_target="tpu_custom_call" | custom-call | tf_op jit(solution)/shard_map/exchange/pallas_call | solution.py:290
  17.2 0.0 copy-done.4
  17.3 60.3 %sums.1 = f32[4,3,312]{2,1,0:T(4,128)S(1)} custom-call(s32[2,512]{1,0:T(2,128)S(1)} %get-tuple-element.13.table, f32[27,4,4,384]{3,2,1,0:T(4,128)S(1)} %get-tuple-element.14.halo, bf16[4,2,312,128]{3,2,1,0:T(8,128)(2,1)S(1)} %get-tuple-element.15.target, f32[16,312]{1,0:T(8,128)S(1)} %get-tuple-element.16.own_bend, ...), custom_call_target="tpu_custom_call" | custom-call | tf_op jit(solution)/shard_map/sums/pallas_call | solution.py:271
  77.6 0.6 copy.13
  (4 shorter events, 0.0 us)
Async XLA Ops:
  0.0 2.2 %copy-start.2 = (f32[312,169]{0,1:T(8,128)S(1)}, f32[312,169]{0,1:T(8,128)}, u32[]{:S(2)}) copy-start(f32[312,169]{0,1:T(8,128)} %param.9) | copy-start | bytes 632740
  0.0 2.4 %copy-start.3 = (f32[1,1,1,4,3,312]{5,3,4,2,1,0:T(4,128)S(1)}, f32[1,1,1,4,3,312]{5,3,4,2,1,0:T(4,128)}, u32[]{:S(2)}) copy-start(f32[1,1,1,4,3,312]{5,3,4,2,1,0:T(4,128)} %param.8) | copy-start | bytes 44932
  0.0 2.4 %copy-start.5 = (s32[1,1,1,16,3]{3,2,4,1,0:T(1,128)S(1)}, s32[1,1,1,16,3]{3,2,4,1,0:T(1,128)}, u32[]{:S(2)}) copy-start(s32[1,1,1,16,3]{3,2,4,1,0:T(1,128)} %param.14) | copy-start | bytes 580
  0.0 3.1 %copy-start.1 = (f32[169]{0:T(256)S(1)}, f32[169]{0:T(256)}, u32[]{:S(2)}) copy-start(f32[169]{0:T(256)} %param.11) | copy-start | bytes 2032
  0.0 3.1 %copy-start = (f32[169,312]{1,0:T(8,128)S(1)}, f32[169,312]{1,0:T(8,128)}, u32[]{:S(2)}) copy-start(f32[169,312]{1,0:T(8,128)} %analysis.1) | copy-start | bytes 632740
  2.2 15.1 %copy-start.4 = (f32[1248]{0:T(1024)S(1)}, f32[1248]{0:T(1024)}, u32[]{:S(2)}) copy-start(f32[1248]{0:T(1024)} %param.13) | copy-start | bytes 14980

commit v2 on v1

v2 whole, which is shorter than its diff:
```python
import functools
import math

import jax
import jax.numpy as jnp
from jax import lax
from jax.experimental import pallas as pl
from jax.experimental.pallas import tpu as pltpu
from jax.sharding import PartitionSpec as P

MESH = pl.DeviceIdType.MESH
F32 = jnp.float32
BF16 = jnp.bfloat16
smooth_sq = 0.25

CELLS = 4
POINTS = 312
RAISED = 1248
SLOTS = 16
LANES = 128
PW = 384
RW = 1280
OWN = 13
LIST = 512
GROUP = 32
DEPTH = 80


def split2(x):
    high = x.astype(BF16)
    return high, (x - high.astype(F32)).astype(BF16)


def split3(x):
    a = x.astype(BF16).astype(F32)
    rest = x - a
    b = rest.astype(BF16).astype(F32)
    return a, b, rest - b


def dot_nt(a, b):
    return lax.dot_general(a, b, (((1,), (1,)), ((), ())), preferred_element_type=F32)


def dot(a, b, precision=None):
    return jnp.dot(a, b, preferred_element_type=F32, precision=precision)


def dot3(a, b_high, b_low):
    high, low = split2(a)
    return dot(high, b_high) + dot(low, b_high) + dot(high, b_low)


def exchange_kernel(
    surface, pairs, count, synthesis, analysis, stiffness, upsample,
    halo, table, target, own_place, own_bend, bend_high, bend_low, up_high, up_low,
    code_s, near_s, far_s, rows_s, own_s, slots_s, raise_s, raise_sem, send_sem, recv_sem,
):
    sizes = [lax.axis_size(a) for a in ("tx", "ty", "tz")]
    here = [lax.axis_index(a) for a in ("tx", "ty", "tz")]
    others = [n for n in range(27) if n != OWN]

    def at(n):
        step = (n // 9 - 1, n // 3 % 3 - 1, n % 3 - 1)
        return tuple(lax.rem(h + d + s, s) for h, d, s in zip(here, step, sizes))

    fetch = pltpu.make_async_copy(upsample, raise_s, raise_sem)
    fetch.start()
    barrier = pltpu.get_barrier_semaphore()
    for n in others:
        pl.semaphore_signal(barrier, inc=1, device_id=at(n), device_id_type=MESH)

    own_s[...] = jnp.zeros((16, PW), F32)
    for c in range(CELLS):
        for k in range(3):
            own_s[4 * c + k : 4 * c + k + 1, :POINTS] = surface[k, c : c + 1, :]
    used = count[0]
    lane = lax.broadcasted_iota(jnp.int32, (1, LANES), 1)
    for c in range(CELLS):
        at_row = 4 * c
        halo[OWN, c, 0:3] = own_s[at_row : at_row + 3, :LANES]
        halo[OWN, c, 3:6] = own_s[at_row : at_row + 3, LANES : 2 * LANES]
        halo[OWN, c, 6:7] = own_s[at_row : at_row + 1, 2 * LANES :] + pltpu.roll(
            own_s[at_row + 1 : at_row + 2, 2 * LANES :], 64, 1
        )
        row = own_s[at_row + 2 : at_row + 3, 2 * LANES :]
        if c < 3:
            slots_s[...] = jnp.full((1, LANES), -1.0, F32)
            slots_s[:, :SLOTS] = pairs[c].astype(F32)
            pair = slots_s[...]
            if c == 1:
                pair = jnp.where(lane < used, pair, -1.0)
            pair = pltpu.roll(jnp.where(lane < SLOTS, pair, 0.0), 64, 1)
            row = row + pair
        halo[OWN, c, 7:8] = row

    pl.semaphore_wait(barrier, 26)

    copies = []
    for n in others:
        copy = pltpu.make_async_remote_copy(
            src_ref=halo.at[OWN],
            dst_ref=halo.at[26 - n],
            send_sem=send_sem.at[n],
            recv_sem=recv_sem.at[26 - n],
            device_id=at(n),
            device_id_type=MESH,
        )
        copy.start()
        copies.append(copy)

    highest = lax.Precision.HIGHEST
    modes = analysis.shape[0]
    diagonal = lax.broadcasted_iota(jnp.int32, (modes, modes), 0) == lax.broadcasted_iota(
        jnp.int32, (modes, modes), 1
    )
    stiff = jnp.sum(jnp.where(diagonal, stiffness[...], 0.0), axis=1, keepdims=True)
    bend = lax.dot_general(
        analysis[...] * stiff, synthesis[...], (((0,), (0,)), ((), ())),
        preferred_element_type=F32, precision=highest,
    )
    bend_high[...], bend_low[...] = split2(bend)
    own = own_s[...]
    own_bend[...] = dot(own[:, :POINTS], bend, highest)
    fetch.wait()
    up_high[:, :RAISED], up_low[:, :RAISED] = split2(raise_s[...])
    up_high[:, RAISED:] = jnp.zeros((POINTS, RW - RAISED), BF16)
    up_low[:, RAISED:] = jnp.zeros((POINTS, RW - RAISED), BF16)
    own_place[...] = own[:, :POINTS]
    ones = jnp.ones((3, PW), F32)
    for c in range(CELLS):
        t = own[4 * c : 4 * c + 3, :]
        norm = jnp.sum(t * t, axis=0, keepdims=True) + smooth_sq
        t1, t2, t3 = split3(t)
        s1, s2, s3 = split3(norm)
        for kind in range(2):
            at_row = 4 * kind
            scale = 1.0 if kind else -2.0
            rows_s[...] = jnp.zeros((LANES, PW), F32)
            for block, part in enumerate((t1, t1, t2, t2, t1, t3)):
                rows_s[8 * block + at_row : 8 * block + at_row + 3, :] = part * scale
            for block in (6, 7, 8):
                rows_s[8 * block + at_row : 8 * block + at_row + 3, :] = -ones if kind else ones
            if not kind:
                rows_s[72:73, :] = s1
                rows_s[73:74, :] = s2
                rows_s[74:75, :] = s3
            target[c, kind] = jnp.transpose(rows_s[...])[:POINTS].astype(BF16)

    for copy in copies:
        copy.wait_recv()

    for ref, k in ((near_s, 0), (code_s, 1), (far_s, 2)):
        ref[...] = jnp.full((LANES, LANES), -1.0, F32)
        for n in range(27):
            ref[n : n + 1, :] = halo[n, k, 7:8, :]
        ref[27:28, :] = halo[OWN, k, 7:8, :]
    place = lax.broadcasted_iota(jnp.int32, (32, LANES), 0)
    place_f = place.astype(F32)
    lane32 = lax.broadcasted_iota(jnp.int32, (32, LANES), 1)
    code, near, far = code_s[:32, :], near_s[:32, :], far_s[:32, :]
    mask = jnp.logical_or(
        jnp.logical_and(place < 27, code == 26.0 - place_f),
        jnp.logical_and(place == 27, code >= 0.0),
    )
    mask = jnp.logical_and(mask, jnp.logical_and(lane32 >= 64, lane32 < 64 + SLOTS))
    value = jnp.where(
        place == 27, near * 128.0 + (code * 4.0 + far), far * 128.0 + (place_f * 4.0 + near)
    )
    taken = mask.astype(F32)
    upper = (
        lax.broadcasted_iota(jnp.int32, (LANES, LANES), 0)
        < lax.broadcasted_iota(jnp.int32, (LANES, LANES), 1)
    ).astype(F32)
    lower = (
        lax.broadcasted_iota(jnp.int32, (32, 32), 1) < lax.broadcasted_iota(jnp.int32, (32, 32), 0)
    ).astype(F32)
    per_row = jnp.broadcast_to(jnp.sum(taken, axis=1, keepdims=True), (32, LANES))
    before = jnp.dot(taken, upper, preferred_element_type=F32)
    above = jnp.dot(lower, per_row, preferred_element_type=F32)
    code_s[:32, :] = jnp.where(mask, before + above, -1.0)
    near_s[:32, :] = value
    spot = jnp.transpose(code_s[...])[64 : 64 + SLOTS]
    value = jnp.transpose(near_s[...])[64 : 64 + SLOTS]
    index = lax.broadcasted_iota(jnp.int32, (SLOTS, LIST), 1).astype(F32)
    listed = jnp.zeros((SLOTS, LIST), F32)
    for n in range(28):
        listed = listed + jnp.where(spot[:, n : n + 1] == index, value[:, n : n + 1], 0.0)
    table[0:1, :] = jnp.sum(listed, axis=0, keepdims=True).astype(jnp.int32)
    total = jnp.sum(jnp.sum(taken, axis=1, keepdims=True), axis=0, keepdims=True)
    table[1:2, :] = jnp.broadcast_to(total, (1, LIST)).astype(jnp.int32)

    for copy in copies:
        copy.wait_send()


def sums_kernel(
    table, halo, target, own_place, own_bend, bend_high, bend_low, up_high, up_low, weight,
    velocity,
    source_s, raised_s, wide0, wide1, forms0, forms1, total_s, operand_s,
):
    count = table[1, 0]
    wide_s, forms_s = (wide0, wide1), (forms0, forms1)
    total_s[...] = jnp.zeros(total_s.shape, F32)
    source_s[...] = jnp.zeros(source_s.shape, F32)
    row8 = lax.broadcasted_iota(jnp.int32, (8, RW), 0)

    def group(g, carry):
        first = g * GROUP
        last = jnp.minimum(first + GROUP, count)

        def pick(e, carry):
            cell = table[0, jnp.minimum(first + e, count - 1)] % 128
            tile = halo[cell // 4, cell % 4]
            for at_row in (0, 4):
                source_s[e, at_row : at_row + 3, :LANES] = tile[0:3]
                source_s[e, at_row : at_row + 3, LANES : 2 * LANES] = tile[3:6]
                source_s[e, at_row : at_row + 1, 2 * LANES :] = tile[6:7]
                source_s[e, at_row + 1 : at_row + 2, 2 * LANES :] = pltpu.roll(tile[6:7], 64, 1)
                source_s[e, at_row + 2 : at_row + 3, 2 * LANES :] = tile[7:8]
            return carry

        lax.fori_loop(0, GROUP, pick, 0)
        picked = source_s[...].reshape(GROUP * 8, PW)[:, :POINTS]
        bent = dot3(picked, bend_high[...], bend_low[...])
        is_pos = lax.broadcasted_iota(jnp.int32, (GROUP * 8, POINTS), 0) % 8 < 4
        carried = jnp.where(is_pos, picked, bent)
        raised = dot3(carried, up_high[...], up_low[...])
        raised_s[...] = raised.reshape(GROUP, 8, RW)

        def prepare(e, slot):
            both = raised_s[jnp.minimum(e, GROUP - 1)] * scale
            for c in range(3):
                wide_s[slot][c] = jnp.broadcast_to(both[c : c + 1, :], (8, RW))
                wide_s[slot][3 + c] = jnp.broadcast_to(both[4 + c : 5 + c, :], (8, RW))
            p1, p2, p3 = split3(both)
            m1, m2, m3 = split3(both * jnp.where(row8 < 4, both, pltpu.roll(both, 4, 0)))
            return jnp.concatenate(
                [p1, p2, p1, p2, p3, p1, m1, m2, m3, jnp.ones((8, RW), F32)], axis=0
            ).astype(BF16)

        def cell_of(e):
            return table[0, jnp.minimum(first + e, LIST - 1)] // 128

        def expand(e, slot, operand, step):
            lanes = slice(step * 256, step * 256 + 256)
            out = jnp.dot(
                target[cell_of(e)].reshape(2 * POINTS, LANES)[:, :DEPTH], operand[:, lanes],
                preferred_element_type=F32,
            )
            forms_s[slot][:, lanes] = out

        def fold2(cell, slot, base, begin, size):
            acc = [None] * size
            for k in range(RW // LANES):
                ln = slice(k * LANES, (k + 1) * LANES)
                ys = [wide_s[slot][c, :, ln] for c in range(3)]
                gs = [wide_s[slot][3 + c, :, ln] for c in range(3)]
                for r in range(size):
                    row = base + 8 * (begin + r)
                    inverse = lax.rsqrt(forms_s[slot][pl.ds(row, 8), ln])
                    factor = forms_s[slot][pl.ds(POINTS + row, 8), ln] * inverse * (inverse * inverse)
                    new = [gs[c] * inverse - ys[c] * factor for c in range(3)] + [factor]
                    acc[r] = new if k == 0 else [a + b for a, b in zip(acc[r], new)]
            for r in range(size):
                row = base + 8 * (begin + r)
                for c in range(4):
                    total_s[cell, c, pl.ds(row, 8), :] += acc[r][c]

        def both_slots(i, carry):
            for half in range(2):
                e = 2 * i + half
                cell = jnp.where(e < last - first, cell_of(e), CELLS)
                operand = prepare(e + 1, 1 - half)
                def chunk(q, carry):
                    base = pl.multiple_of(q * 104, 8)
                    for kind in range(2):
                        out = jnp.dot(target[cell_of(e + 1), kind, pl.ds(base, 104), :][:, :DEPTH], operand_s[...], preferred_element_type=F32)
                        forms_s[1 - half][pl.ds(kind * POINTS + base, 104), :] = out
                    for begin in range(0, 13, 3):
                        fold2(cell, half, base, begin, min(3, 13 - begin))
                    return carry
                operand_s[...] = operand
                lax.fori_loop(0, 3, chunk, 0)
            return carry

        scale = jnp.where(row8 < 4, 1.0, weight[...])
        operand = prepare(0, 0)
        for step in range(5):
            expand(0, 0, operand, step)
        lax.fori_loop(0, (last - first + 1) // 2, both_slots, 0)
        return carry

    lax.fori_loop(0, (count + GROUP - 1) // GROUP, group, 0)

    ones = jnp.ones((8, LANES), BF16)

    def reduced(x):
        high, low = split2(x)
        return (dot_nt(ones, high) + dot_nt(ones, low))[0:1, :]

    for c in range(CELLS):
        weight_sum = reduced(total_s[c, 3])
        for k in range(3):
            row = 4 * c + k
            place = own_place[row : row + 1, :]
            velocity[k, c : c + 1, :] = (
                0.25 * own_bend[row : row + 1, :]
                + reduced(total_s[c, k])
                + place * weight_sum
            )


VMEM = pl.BlockSpec(memory_space=pltpu.VMEM)
SMEM = pl.BlockSpec(memory_space=pltpu.SMEM)


def sums(table, halo, target, own_place, own_bend, bend_high, bend_low, up_high, up_low, weight):
    return pl.pallas_call(
        sums_kernel,
        out_shape=jax.ShapeDtypeStruct((3, CELLS, POINTS), F32),
        in_specs=[SMEM] + [VMEM] * 9,
        out_specs=VMEM,
        scratch_shapes=[
            pltpu.VMEM((GROUP, 8, PW), F32),
            pltpu.VMEM((GROUP, 8, RW), F32),
            pltpu.VMEM((6, 8, RW), F32),
            pltpu.VMEM((6, 8, RW), F32),
            pltpu.VMEM((2 * POINTS, RW), F32),
            pltpu.VMEM((2 * POINTS, RW), F32),
            pltpu.VMEM((CELLS + 1, 4, POINTS, LANES), F32),
            pltpu.VMEM((DEPTH, RW), BF16),
        ],
        compiler_params=pltpu.CompilerParams(vmem_limit_bytes=40 * 2**20),
        name="sums",
    )(table, halo, target, own_place, own_bend, bend_high, bend_low, up_high, up_low, weight)


def shards(surface, synthesis, analysis, stiffness, upsample, quad_weight, near_pairs, pair_count):
    outs = pl.pallas_call(
        exchange_kernel,
        out_shape=(
            jax.ShapeDtypeStruct((27, CELLS, 8, LANES), F32),
            jax.ShapeDtypeStruct((2, LIST), jnp.int32),
            jax.ShapeDtypeStruct((CELLS, 2, POINTS, LANES), BF16),
            jax.ShapeDtypeStruct((16, POINTS), F32),
            jax.ShapeDtypeStruct((16, POINTS), F32),
            jax.ShapeDtypeStruct((POINTS, POINTS), BF16),
            jax.ShapeDtypeStruct((POINTS, POINTS), BF16),
            jax.ShapeDtypeStruct((POINTS, RW), BF16),
            jax.ShapeDtypeStruct((POINTS, RW), BF16),
        ),
        in_specs=[VMEM, VMEM, SMEM] + [VMEM] * 3 + [pl.BlockSpec(memory_space=pltpu.HBM)],
        out_specs=[VMEM] * 9,
        scratch_shapes=[
            pltpu.VMEM((LANES, LANES), F32),
            pltpu.VMEM((LANES, LANES), F32),
            pltpu.VMEM((LANES, LANES), F32),
            pltpu.VMEM((LANES, PW), F32),
            pltpu.VMEM((16, PW), F32),
            pltpu.VMEM((1, LANES), F32),
            pltpu.VMEM((POINTS, RAISED), F32),
            pltpu.SemaphoreType.DMA,
            pltpu.SemaphoreType.DMA((27,)),
            pltpu.SemaphoreType.DMA((27,)),
        ],
        compiler_params=pltpu.CompilerParams(
            collective_id=0, has_side_effects=True, vmem_limit_bytes=40 * 2**20
        ),
        name="exchange",
    )(
        jnp.swapaxes(surface[0, 0, 0], 0, 1), near_pairs[0, 0, 0].T[:, None, :], pair_count.reshape(1),
        synthesis.T, analysis, stiffness[None, :], upsample.T,
    )
    halo, table, *prepared = outs
    weight = jnp.pad(quad_weight * (1.0 / math.sqrt(RAISED)), (0, RW - RAISED))[None, :]
    velocity = sums(table, halo, *prepared, weight)
    return jnp.swapaxes(velocity, 0, 1)[None, None, None]


def solution(mesh):
    return jax.shard_map(
        shards,
        mesh=mesh,
        in_specs=(
            P("tx", "ty", "tz", None, None, None),
            P(),
            P(),
            P(),
            P(),
            P(),
            P("tx", "ty", "tz", None, None),
            P("tx", "ty", "tz"),
        ),
        out_specs=P("tx", "ty", "tz", None, None, None),
        check_vma=False,
    )
```

time: 78.4 us -> 59.8 us (0.76)
  the two profiles are of different devices: /device:TPU:33 before, /device:TPU:104 now
where the time goes in v2:
time: 59.8 us; the launch traced here: 59.5 us
  Pallas kernels  52.7 us (88%)
  local copies, waits for them, and re-layouts  5.41 us (9%)
  other arithmetic  0.7 us (1%)
  between operations  0.68 us (1%)
    pallas_call x1, Pallas kernels, sums(): pl.pallas_call(sums_kernel, out_shape=jax.ShapeDtypeStruct((3, CELLS, POI...  40.9 us
    pallas_call x1, Pallas kernels, shards(): pl.pallas_call(exchange_kernel, out_shape=(jax.ShapeDtypeStruct((27, CELL...  11.9 us
    unnamed x11, local copies, waits for them, and re-layouts  5.4 us

profile of v2, /device:TPU:104, one launch (start us, length us, event | category | flops | bytes accessed | tf_op | source)
XLA Modules:
  0.0 59.5 jit_solution(16740221006048309523)
XLA Ops:
  0.7 0.7 %copy.12 = s32[1,1,1,16,3]{3,4,2,1,0:T(4,128)S(1)} copy(s32[1,1,1,16,3]{3,2,4,1,0:T(1,128)} %param.14) | data formatting | bytes 384
  1.3 0.7 %broadcast_multiply_fusion = f32[1248]{0:T(1024)S(1)} fusion(f32[1248]{0:T(1024)} %param.13), kind=kLoop, calls=%fused_computation | loop fusion | flops 1248 | bytes 9984 | tf_op jit(solution)/shard_map/mul | solution.py:376
  2.1 0.0 copy-start
  2.1 1.4 %copy-done = f32[1248,312]{0,1:T(8,128)S(1)} copy-done((f32[1248,312]{0,1:T(8,128)S(1)}, f32[1248,312]{0,1:T(8,128)}, u32[]{:S(2)}) %copy-start) | copy-done | bytes 1557528
  3.5 0.0 copy-start.1
  3.5 1.0 %copy-done.1 = f32[312,169]{0,1:T(8,128)S(1)} copy-done((f32[312,169]{0,1:T(8,128)S(1)}, f32[312,169]{0,1:T(8,128)}, u32[]{:S(2)}) %copy-start.1) | copy-done | bytes 210936
  4.4 0.0 copy-start.2
  4.4 1.0 %copy-done.2 = f32[169,312]{1,0:T(8,128)S(1)} copy-done((f32[169,312]{1,0:T(8,128)S(1)}, f32[169,312]{1,0:T(8,128)}, u32[]{:S(2)}) %copy-start.2) | copy-done | bytes 210936
  5.4 0.0 copy-start.3
  5.4 0.7 %copy-done.3 = f32[1,1,1,4,3,312]{5,3,4,2,1,0:T(4,128)S(1)} copy-done((f32[1,1,1,4,3,312]{5,3,4,2,1,0:T(4,128)S(1)}, f32[1,1,1,4,3,312]{5,3,4,2,1,0:T(4,128)}, u32[]{:S(2)}) %copy-start.3) | copy-done | bytes 15000
  6.1 0.0 copy-start.4
  6.1 0.7 %copy-done.4 = f32[169]{0:T(256)S(1)} copy-done((f32[169]{0:T(256)S(1)}, f32[169]{0:T(256)}, u32[]{:S(2)}) %copy-start.4) | copy-done | bytes 700
  6.8 11.9 %exchange.1 = (f32[27,4,8,128]{3,2,1,0:T(8,128)S(1)}, s32[2,512]{1,0:T(2,128)S(1)}, bf16[4,2,312,128]{3,2,1,0:T(8,128)(2,1)S(1)}, f32[16,312]{1,0:T(8,128)S(1)},...) custom-call(f32[3,4,312]{2,1,0:T(4,128)S(1)} %bitcast.20, ...), custom_call_target="tpu_custom_call" | custom-call | tf_op jit(solution)/shard_map/exchange/pallas_call | solution.py:340
  18.6 40.9 %sums.1 = f32[3,4,312]{2,1,0:T(4,128)} custom-call(s32[2,512]{1,0:T(2,128)S(1)} %get-tuple-element.14.table, f32[27,4,8,128]{3,2,1,0:T(8,128)S(1)} %get-tuple-element.15.halo, bf16[4,2,312,128]{3,2,1,0:T(8,128)(2,1)S(1)} %get-tuple-element.16.target, f32[16,312]{1,0:T(8,128)S(1)} %get-tuple-element.17.own_place, f32[16,312]{1,0:T(8,128)S(1)} %get-tuple-element.18.own_bend, ...), custom_call_target="tpu_custom_call" | custom-call | tf_op jit(solution)/shard_map/sums/pallas_call | solution.py:319
  (3 shorter events, 0.0 us)
Async XLA Ops:
  2.1 1.4 %copy-start = (f32[1248,312]{0,1:T(8,128)S(1)}, f32[1248,312]{0,1:T(8,128)}, u32[]{:S(2)}) copy-start(f32[1248,312]{0,1:T(8,128)} %param.12) | copy-start | bytes 4672516
  3.5 1.0 %copy-start.1 = (f32[312,169]{0,1:T(8,128)S(1)}, f32[312,169]{0,1:T(8,128)}, u32[]{:S(2)}) copy-start(f32[312,169]{0,1:T(8,128)} %param.9) | copy-start | bytes 632740
  4.4 1.0 %copy-start.2 = (f32[169,312]{1,0:T(8,128)S(1)}, f32[169,312]{1,0:T(8,128)}, u32[]{:S(2)}) copy-start(f32[169,312]{1,0:T(8,128)} %analysis.1) | copy-start | bytes 632740
  5.4 0.7 %copy-start.3 = (f32[1,1,1,4,3,312]{5,3,4,2,1,0:T(4,128)S(1)}, f32[1,1,1,4,3,312]{5,3,4,2,1,0:T(4,128)}, u32[]{:S(2)}) copy-start(f32[1,1,1,4,3,312]{5,3,4,2,1,0:T(4,128)} %param.8) | copy-start | bytes 44932
  6.1 0.7 %copy-start.4 = (f32[169]{0:T(256)S(1)}, f32[169]{0:T(256)}, u32[]{:S(2)}) copy-start(f32[169]{0:T(256)} %param.11) | copy-start | bytes 2032

commit v3 on v2

v3 whole, which is shorter than its diff:
```python
import functools
import math

import jax
import jax.numpy as jnp
from jax import lax
from jax.experimental import pallas as pl
from jax.experimental.pallas import tpu as pltpu
from jax.sharding import PartitionSpec as P

MESH = pl.DeviceIdType.MESH
F32 = jnp.float32
BF16 = jnp.bfloat16
smooth_sq = 0.25

CELLS = 4
POINTS = 312
RAISED = 1248
MODES = 169
SLOTS = 16
LANES = 128
PW = 384
RW = 1280
VMEM_BYTES = 63 * 2**20
OWN = 13
LIST = 512
CHUNKS = 3
CHUNK = POINTS // CHUNKS
GROUP = 32
DEPTH = 80


def split2(x):
    high = x.astype(BF16)
    return high, (x - high.astype(F32)).astype(BF16)


def split3(x):
    a = x.astype(BF16).astype(F32)
    rest = x - a
    b = rest.astype(BF16).astype(F32)
    return a, b, rest - b


def dot_nt(a, b):
    return lax.dot_general(a, b, (((1,), (1,)), ((), ())), preferred_element_type=F32)


def dot(a, b, precision=None):
    return jnp.dot(a, b, preferred_element_type=F32, precision=precision)


def split_rows(x):
    high, low = split2(x[:, :256])
    lane = lax.broadcasted_iota(jnp.int32, (x.shape[0], LANES), 1)
    rest = jnp.where(lane < 64, x[:, 256:], 0.0)
    rest_high = rest.astype(BF16).astype(F32)
    both = rest_high + pltpu.roll(rest - rest_high, 64, 1)
    return jnp.concatenate([high, low, high, both.astype(BF16), rest_high.astype(BF16)], axis=1)


def split_columns(place, x):
    width = x.shape[1]
    place[...] = jnp.zeros(place.shape, BF16)
    place[0:256, :width], place[256:512, :width] = split2(x[:256])
    rest = jnp.concatenate([x[256:], jnp.zeros((64 - (POINTS - 256), width), F32)], axis=0)
    high, low = split2(rest)
    place[512:576, :width] = high
    place[576:640, :width] = high
    place[640:704, :width] = low


def split_dot(x, place):
    whole = jnp.concatenate([place[0:256], place[0:256], place[256:512], place[512:768]], axis=0)
    return dot(x, whole)


def exchange_kernel(
    count_h, surface_h, pairs_h, synthesis_h, analysis_h, stiffness_h, upsample_h, weight_h,
    halo_h, table_h, target_h, own_h, bend_h, up_h, weight_out_h,
    halo, table, target, own_v, bend_v, up_v, weight,
    code_s, near_s, far_s, rows_s, own_s, slots_s,
    surface, pairs, synthesis, analysis, stiffness, upsample, weight_s, count,
    fetch_sem, store_sem, send_sem, recv_sem,
):
    sizes = [lax.axis_size(a) for a in ("tx", "ty", "tz")]
    here = [lax.axis_index(a) for a in ("tx", "ty", "tz")]
    others = [n for n in range(27) if n != OWN]

    def at(n):
        step = (n // 9 - 1, n // 3 % 3 - 1, n % 3 - 1)
        return tuple(lax.rem(h + d + s, s) for h, d, s in zip(here, step, sizes))

    fetches = []
    for i, (source, place) in enumerate((
        (surface_h, surface), (pairs_h, pairs), (count_h, count), (synthesis_h, synthesis),
        (analysis_h, analysis), (stiffness_h, stiffness), (upsample_h, upsample),
        (weight_h, weight_s),
    )):
        fetch = pltpu.make_async_copy(source, place, fetch_sem.at[i])
        fetch.start()
        fetches.append(fetch)
    barrier = pltpu.get_barrier_semaphore()
    for n in others:
        pl.semaphore_signal(barrier, inc=1, device_id=at(n), device_id_type=MESH)

    own_s[...] = jnp.zeros((16, PW), F32)
    for fetch in fetches[:3]:
        fetch.wait()
    for c in range(CELLS):
        for k in range(3):
            own_s[4 * c + k : 4 * c + k + 1, :POINTS] = surface[k, c : c + 1, :]
    used = count[0, 0, 0]
    lane = lax.broadcasted_iota(jnp.int32, (1, LANES), 1)
    for c in range(CELLS):
        at_row = 4 * c
        halo[4 * OWN + c, 0:3] = own_s[at_row : at_row + 3, :LANES]
        halo[4 * OWN + c, 3:6] = own_s[at_row : at_row + 3, LANES : 2 * LANES]
        halo[4 * OWN + c, 6:7] = own_s[at_row : at_row + 1, 2 * LANES :] + pltpu.roll(
            own_s[at_row + 1 : at_row + 2, 2 * LANES :], 64, 1
        )
        row = own_s[at_row + 2 : at_row + 3, 2 * LANES :]
        if c < 3:
            slots_s[...] = jnp.full((1, LANES), -1.0, F32)
            slots_s[:, :SLOTS] = pairs[0, 0, c].astype(F32)
            pair = slots_s[...]
            if c == 1:
                pair = jnp.where(lane < used, pair, -1.0)
            pair = pltpu.roll(jnp.where(lane < SLOTS, pair, 0.0), 64, 1)
            row = row + pair
        halo[4 * OWN + c, 7:8] = row

    pl.semaphore_wait(barrier, 26)

    copies = []
    for n in others:
        copy = pltpu.make_async_remote_copy(
            src_ref=halo.at[pl.ds(4 * OWN, CELLS)],
            dst_ref=halo.at[pl.ds(4 * (26 - n), CELLS)],
            send_sem=send_sem.at[n],
            recv_sem=recv_sem.at[26 - n],
            device_id=at(n),
            device_id_type=MESH,
        )
        copy.start()
        copies.append(copy)

    highest = lax.Precision.HIGHEST
    for fetch in fetches[3:]:
        fetch.wait()
    modes = analysis.shape[0]
    diagonal = lax.broadcasted_iota(jnp.int32, (modes, modes), 0) == lax.broadcasted_iota(
        jnp.int32, (modes, modes), 1
    )
    stiff = jnp.sum(jnp.where(diagonal, stiffness[...], 0.0), axis=1, keepdims=True)
    bend = lax.dot_general(
        analysis[...] * stiff, synthesis[...], (((0,), (0,)), ((), ())),
        preferred_element_type=F32, precision=highest,
    )
    split_columns(bend_v, bend)
    own = own_s[...]
    own_v[1, :, :POINTS] = dot(own[:, :POINTS], bend, highest)
    split_columns(up_v, upsample[...])
    own_v[0] = own
    weight[...] = jnp.ones((8, RW), F32)
    weight[4:8, :RAISED] = jnp.broadcast_to(weight_s[...][None, :] * (1.0 / math.sqrt(RAISED)), (4, RAISED))
    ones = jnp.ones((3, PW), F32)
    for c in range(CELLS):
        t = own[4 * c : 4 * c + 3, :]
        norm = jnp.sum(t * t, axis=0, keepdims=True) + smooth_sq
        t1, t2, t3 = split3(t)
        s1, s2, s3 = split3(norm)
        forms = []
        for kind in range(2):
            at_row = 4 * kind
            scale = 1.0 if kind else -2.0
            rows_s[...] = jnp.zeros((LANES, PW), F32)
            for block, part in enumerate((t1, t1, t2, t2, t1, t3)):
                rows_s[8 * block + at_row : 8 * block + at_row + 3, :] = part * scale
            for block in (6, 7, 8):
                rows_s[8 * block + at_row : 8 * block + at_row + 3, :] = -ones if kind else ones
            if not kind:
                rows_s[72:73, :] = s1
                rows_s[73:74, :] = s2
                rows_s[74:75, :] = s3
            forms.append(jnp.transpose(rows_s[...]))
        for q in range(CHUNKS):
            rows = slice(q * CHUNK, (q + 1) * CHUNK)
            target[c, q] = jnp.concatenate([forms[0][rows], forms[1][rows]], axis=0).astype(BF16)
    stores = []

    def store(place, out):
        copy = pltpu.make_async_copy(place, out, store_sem.at[len(stores)])
        copy.start()
        stores.append(copy)

    store(target, target_h)
    store(own_v, own_h)
    store(bend_v, bend_h)
    store(up_v, up_h)
    store(weight, weight_out_h)

    for copy in copies:
        copy.wait_recv()
    store(halo, halo_h)

    for ref, k in ((near_s, 0), (code_s, 1), (far_s, 2)):
        ref[...] = jnp.full((LANES, LANES), -1.0, F32)
        for n in range(27):
            ref[n : n + 1, :] = halo[4 * n + k, 7:8, :]
        ref[27:28, :] = halo[4 * OWN + k, 7:8, :]
    place = lax.broadcasted_iota(jnp.int32, (32, LANES), 0)
    place_f = place.astype(F32)
    lane32 = lax.broadcasted_iota(jnp.int32, (32, LANES), 1)
    code, near, far = code_s[:32, :], near_s[:32, :], far_s[:32, :]
    mask = jnp.logical_or(
        jnp.logical_and(place < 27, code == 26.0 - place_f),
        jnp.logical_and(place == 27, code >= 0.0),
    )
    mask = jnp.logical_and(mask, jnp.logical_and(lane32 >= 64, lane32 < 64 + SLOTS))
    value = jnp.where(
        place == 27, near * 128.0 + (code * 4.0 + far), far * 128.0 + (place_f * 4.0 + near)
    )
    taken = mask.astype(F32)
    upper = (
        lax.broadcasted_iota(jnp.int32, (LANES, LANES), 0)
        < lax.broadcasted_iota(jnp.int32, (LANES, LANES), 1)
    ).astype(F32)
    lower = (
        lax.broadcasted_iota(jnp.int32, (32, 32), 1) < lax.broadcasted_iota(jnp.int32, (32, 32), 0)
    ).astype(F32)
    per_row = jnp.broadcast_to(jnp.sum(taken, axis=1, keepdims=True), (32, LANES))
    before = jnp.dot(taken, upper, preferred_element_type=F32)
    above = jnp.dot(lower, per_row, preferred_element_type=F32)
    code_s[:32, :] = jnp.where(mask, before + above, -1.0)
    near_s[:32, :] = value
    spot = jnp.transpose(code_s[...])[64 : 64 + SLOTS]
    value = jnp.transpose(near_s[...])[64 : 64 + SLOTS]
    index = lax.broadcasted_iota(jnp.int32, (SLOTS, LIST), 1).astype(F32)
    listed = jnp.zeros((SLOTS, LIST), F32)
    for n in range(28):
        listed = listed + jnp.where(spot[:, n : n + 1] == index, value[:, n : n + 1], 0.0)
    table[0:1, :] = jnp.sum(listed, axis=0, keepdims=True).astype(jnp.int32)
    total = jnp.sum(jnp.sum(taken, axis=1, keepdims=True), axis=0, keepdims=True)
    table[1:2, :] = jnp.broadcast_to(total, (1, LIST)).astype(jnp.int32)

    store(table, table_h)
    for copy in stores:
        copy.wait()
    for copy in copies:
        copy.wait_send()


def sums_kernel(
    table_h, halo_h, target_h, own_h, bend_h, up_h, weight_h,
    velocity,
    table, halo, target, own, bend, up, weight, fetch_sem,
    source_s, raised_s, wide0, wide1, forms0, forms1, total_s, operand_s,
):
    fetches = []
    for i, (source, place) in enumerate((
        (table_h, table), (halo_h, halo), (bend_h, bend), (up_h, up),
        (weight_h, weight), (target_h, target), (own_h, own),
    )):
        fetch = pltpu.make_async_copy(source, place, fetch_sem.at[i])
        fetch.start()
        fetches.append(fetch)
    wide_s, forms_s = (wide0, wide1), (forms0, forms1)
    total_s[...] = jnp.zeros(total_s.shape, F32)
    source_s[...] = jnp.zeros(source_s.shape, F32)
    for fetch in fetches:
        fetch.wait()
    count = table[1, 0]
    row8 = lax.broadcasted_iota(jnp.int32, (8, RW), 0)

    def group(g, carry):
        first = g * GROUP
        last = jnp.minimum(first + GROUP, count)

        for e in range(GROUP):
            tile = halo[table[0, first + e] % 128]
            at_row = e % 2 * 4
            source_s[e // 2, at_row : at_row + 3, :LANES] = tile[0:3]
            source_s[e // 2, at_row : at_row + 3, LANES : 2 * LANES] = tile[3:6]
            source_s[e // 2, at_row : at_row + 1, 2 * LANES :] = tile[6:7]
            source_s[e // 2, at_row + 1 : at_row + 2, 2 * LANES :] = pltpu.roll(tile[6:7], 64, 1)
            source_s[e // 2, at_row + 2 : at_row + 3, 2 * LANES :] = tile[7:8]
        places = split_rows(source_s[...].reshape(GROUP * 4, PW))
        bent = split_rows(split_dot(places, bend))
        raised = split_dot(jnp.concatenate([places, bent], axis=0), up)
        raised_s[...] = raised.reshape(2, GROUP // 2, 8, RW)

        def prepare(block, odd, slot):
            block = jnp.minimum(block, GROUP // 2 - 1)
            places, forces = raised_s[0, block], raised_s[1, block]
            if odd:
                places = pltpu.roll(places, 4, 0)
            else:
                forces = pltpu.roll(forces, 4, 0)
            both = jnp.where(row8 < 4, places, forces) * weight[...]
            for c in range(3):
                wide_s[slot][c] = jnp.broadcast_to(both[c : c + 1, :], (8, RW))
                wide_s[slot][3 + c] = jnp.broadcast_to(both[4 + c : 5 + c, :], (8, RW))
            p1, p2, p3 = split3(both)
            m1, m2, m3 = split3(both * jnp.where(row8 < 4, both, pltpu.roll(both, 4, 0)))
            operand_s[...] = jnp.concatenate(
                [p1, p2, p1, p2, p3, p1, m1, m2, m3, jnp.ones((8, RW), F32)], axis=0
            ).astype(BF16)

        def cell_of(e):
            return table[0, first + e] // 128

        def expand(cell, slot, q):
            forms_s[slot][q] = dot(target[cell, q][:, :DEPTH], operand_s[...])

        def fold(cell, slot, q, begin, size):
            acc = [None] * size
            for k in range(RW // LANES):
                ln = slice(k * LANES, (k + 1) * LANES)
                ys = [wide_s[slot][c, :, ln] for c in range(3)]
                gs = [wide_s[slot][3 + c, :, ln] for c in range(3)]
                for r in range(size):
                    row = 8 * (begin + r)
                    inverse = lax.rsqrt(forms_s[slot][q, row : row + 8, ln])
                    along = forms_s[slot][q, CHUNK + row : CHUNK + row + 8, ln]
                    factor = along * inverse * (inverse * inverse)
                    new = [gs[c] * inverse - ys[c] * factor for c in range(3)] + [factor]
                    acc[r] = new if k == 0 else [a + b for a, b in zip(acc[r], new)]
            for r in range(size):
                row = 8 * (begin + r)
                for c in range(4):
                    total_s[cell, c, q, row : row + 8, :] += acc[r][c]

        def two(i, carry):
            for half in range(2):
                e = 2 * i + half
                cell = jnp.where(e < last - first, cell_of(e), CELLS)
                later = cell_of(e + 1)
                prepare(i + half, 1 - half, 1 - half)

                def chunk(q, carry):
                    expand(later, 1 - half, q)
                    for begin in range(0, CHUNK // 8, 3):
                        fold(cell, half, q, begin, min(3, CHUNK // 8 - begin))
                    return carry

                lax.fori_loop(0, CHUNKS, chunk, 0)
            return carry

        prepare(0, 0, 0)
        for q in range(CHUNKS):
            expand(cell_of(0), 0, q)
        lax.fori_loop(0, (last - first + 1) // 2, two, 0)
        return carry

    lax.fori_loop(0, (count + GROUP - 1) // GROUP, group, 0)

    ones = jnp.ones((8, LANES), BF16)

    def reduced(x):
        high, low = split2(x)
        return (dot_nt(ones, high) + dot_nt(ones, low))[0:1, :]

    for c in range(CELLS):
        weight_sum = reduced(total_s[c, 3].reshape(POINTS, LANES))
        for k in range(3):
            row = 4 * c + k
            place = own[0, row : row + 1, :POINTS]
            velocity[k, c : c + 1, :] = (
                0.25 * own[1, row : row + 1, :POINTS]
                + reduced(total_s[c, k].reshape(POINTS, LANES))
                + place * weight_sum
            )


HBM = pl.BlockSpec(memory_space=pltpu.HBM)

HANDED = (
    ((27 * CELLS, 8, LANES), F32),
    ((2, LIST), jnp.int32),
    ((CELLS, CHUNKS, 2 * CHUNK, LANES), BF16),
    ((2, 16, PW), F32),
    ((768, PW), BF16),
    ((768, RW), BF16),
    ((8, RW), F32),
)


def sums(halo, table, target, own, bend, up, weight):
    held = [pltpu.VMEM(*h) for h in HANDED]
    return pl.pallas_call(
        sums_kernel,
        out_shape=jax.ShapeDtypeStruct((3, CELLS, POINTS), F32),
        in_specs=[HBM] * 7,
        out_specs=pl.BlockSpec(memory_space=pltpu.VMEM),
        scratch_shapes=[
            pltpu.SMEM((2, LIST), jnp.int32),
            held[0],
            *held[2:],
            pltpu.SemaphoreType.DMA((7,)),
            pltpu.VMEM((GROUP // 2, 8, PW), F32),
            pltpu.VMEM((2, GROUP // 2, 8, RW), F32),
            pltpu.VMEM((6, 8, RW), F32),
            pltpu.VMEM((6, 8, RW), F32),
            pltpu.VMEM((CHUNKS, 2 * CHUNK, RW), F32),
            pltpu.VMEM((CHUNKS, 2 * CHUNK, RW), F32),
            pltpu.VMEM((CELLS + 1, 4, CHUNKS, CHUNK, LANES), F32),
            pltpu.VMEM((DEPTH, RW), BF16),
        ],
        compiler_params=pltpu.CompilerParams(vmem_limit_bytes=VMEM_BYTES),
        name="sums",
    )(table, halo, target, own, bend, up, weight)


def shards(surface, synthesis, analysis, stiffness, upsample, quad_weight, near_pairs, pair_count):
    outs = pl.pallas_call(
        exchange_kernel,
        out_shape=[jax.ShapeDtypeStruct(*h) for h in HANDED],
        in_specs=[HBM] * 8,
        out_specs=[HBM] * 7,
        scratch_shapes=[pltpu.VMEM(*h) for h in HANDED]
        + [
            pltpu.VMEM((LANES, LANES), F32),
            pltpu.VMEM((LANES, LANES), F32),
            pltpu.VMEM((LANES, LANES), F32),
            pltpu.VMEM((LANES, PW), F32),
            pltpu.VMEM((16, PW), F32),
            pltpu.VMEM((1, LANES), F32),
            pltpu.VMEM((3, CELLS, POINTS), F32),
            pltpu.VMEM((1, 1, 3, 1, SLOTS), jnp.int32),
            pltpu.VMEM((MODES, POINTS), F32),
            pltpu.VMEM((MODES, POINTS), F32),
            pltpu.VMEM((1, MODES), F32),
            pltpu.VMEM((POINTS, RAISED), F32),
            pltpu.VMEM((RAISED,), F32),
            pltpu.SMEM((1, 1, 1), jnp.int32),
            pltpu.SemaphoreType.DMA((8,)),
            pltpu.SemaphoreType.DMA((7,)),
            pltpu.SemaphoreType.DMA((27,)),
            pltpu.SemaphoreType.DMA((27,)),
        ],
        compiler_params=pltpu.CompilerParams(
            collective_id=0, has_side_effects=True, vmem_limit_bytes=VMEM_BYTES
        ),
        name="exchange",
    )(
        pair_count, jnp.swapaxes(surface[0, 0, 0], 0, 1), near_pairs.transpose(0, 1, 4, 2, 3),
        synthesis.T, analysis, stiffness[None, :], upsample.T, quad_weight,
    )
    velocity = sums(*outs)
    return jnp.swapaxes(velocity, 0, 1)[None, None, None]


def solution(mesh):
    return jax.shard_map(
        shards,
        mesh=mesh,
        in_specs=(
            P("tx", "ty", "tz", None, None, None),
            P(),
            P(),
            P(),
            P(),
            P(),
            P("tx", "ty", "tz", None, None),
            P("tx", "ty", "tz"),
        ),
        out_specs=P("tx", "ty", "tz", None, None, None),
        check_vma=False,
    )
```

time: 59.8 us -> 54 us (0.903)
  the two profiles are of different devices: /device:TPU:104 before, /device:TPU:152 now
where the time goes in v3:
time: 54 us; the launch traced here: 53.8 us
  Pallas kernels  53.2 us (99%)
  between operations  0.66 us (1%)
    pallas_call x1, Pallas kernels, sums(): pl.pallas_call(sums_kernel, out_shape=jax.ShapeDtypeStruct((3, CELLS, POI...  41.1 us
    pallas_call x1, Pallas kernels, shards(): pl.pallas_call(exchange_kernel, out_shape=[jax.ShapeDtypeStruct(*h) for h...  12.1 us

profile of v3, /device:TPU:152, one launch (start us, length us, event | category | flops | bytes accessed | tf_op | source)
XLA Modules:
  0.0 53.8 jit_solution(6491823064007156214)
XLA Ops:
  0.7 12.1 %exchange.1 = (f32[108,8,128]{2,1,0:T(8,128)}, s32[2,512]{1,0:T(2,128)}, bf16[4,3,208,128]{3,2,1,0:T(8,128)(2,1)}, f32[2,16,384]{2,1,0:T(8,128)}, bf16[768,384]{...) custom-call(s32[1,1,1]{2,1,0:T(1,128)S(6)} %copy.9.count_h, f32[3,4,312]{2,1,0:T(4,128)} %bitcast.12, ...), custom_call_target="tpu_custom_call" | custom-call | tf_op jit(solution)/shard_map/exchange/pallas_call | solution.py:416
  12.8 41.1 %sums.1 = f32[3,4,312]{2,1,0:T(4,128)} custom-call(s32[2,512]{1,0:T(2,128)} %get-tuple-element.12.table_h, f32[108,8,128]{2,1,0:T(8,128)} %get-tuple-element.13.halo_h, bf16[4,3,208,128]{3,2,1,0:T(8,128)(2,1)} %get-tuple-element.14.target_h, f32[2,16,384]{2,1,0:T(8,128)} %get-tuple-element.15.own_h, bf16[768,384]{1,0:T(8,128)(2,1)} %get-tuple-element.16.bend_h, ...), custom_call_target="tpu_custom_call" | custom-call | tf_op jit(solution)/shard_map/sums/pallas_call | solution.py:391

commit v4 on v3

--- a/solution.py
+++ b/solution.py
@@ -87,9 +87,28 @@
     here = [lax.axis_index(a) for a in ("tx", "ty", "tz")]
     others = [n for n in range(27) if n != OWN]
 
+    def step(n):
+        return (n // 9 - 1, n // 3 % 3 - 1, n % 3 - 1)
+
     def at(n):
-        step = (n // 9 - 1, n // 3 % 3 - 1, n % 3 - 1)
-        return tuple(lax.rem(h + d + s, s) for h, d, s in zip(here, step, sizes))
+        return tuple(lax.rem(h + d + s, s) for h, d, s in zip(here, step(n), sizes))
+
+    def when_inside(n, act):
+        inside = [
+            jnp.logical_and(h + d >= 0, h + d < s)
+            for h, d, s in zip(here, step(n), sizes) if d
+        ]
+        pl.when(functools.reduce(jnp.logical_and, inside))(act)
+
+    def to(n):
+        return pltpu.make_async_remote_copy(
+            src_ref=halo.at[pl.ds(4 * OWN, CELLS)],
+            dst_ref=halo.at[pl.ds(4 * (26 - n), CELLS)],
+            send_sem=send_sem.at[n],
+            recv_sem=recv_sem.at[26 - n],
+            device_id=at(n),
+            device_id_type=MESH,
+        )
 
     fetches = []
     for i, (source, place) in enumerate((
@@ -101,8 +120,11 @@
         fetch.start()
         fetches.append(fetch)
     barrier = pltpu.get_barrier_semaphore()
+    halo[...] = jnp.full(halo.shape, -1.0, F32)
     for n in others:
-        pl.semaphore_signal(barrier, inc=1, device_id=at(n), device_id_type=MESH)
+        when_inside(n, lambda n=n: pl.semaphore_signal(
+            barrier, inc=1, device_id=at(n), device_id_type=MESH
+        ))
 
     own_s[...] = jnp.zeros((16, PW), F32)
     for fetch in fetches[:3]:
@@ -130,20 +152,12 @@
             row = row + pair
         halo[4 * OWN + c, 7:8] = row
 
-    pl.semaphore_wait(barrier, 26)
-
-    copies = []
+    present = 1
+    for h, s in zip(here, sizes):
+        present = present * (1 + jnp.where(h > 0, 1, 0) + jnp.where(h < s - 1, 1, 0))
+    pl.semaphore_wait(barrier, present - 1)
     for n in others:
-        copy = pltpu.make_async_remote_copy(
-            src_ref=halo.at[pl.ds(4 * OWN, CELLS)],
-            dst_ref=halo.at[pl.ds(4 * (26 - n), CELLS)],
-            send_sem=send_sem.at[n],
-            recv_sem=recv_sem.at[26 - n],
-            device_id=at(n),
-            device_id_type=MESH,
-        )
-        copy.start()
-        copies.append(copy)
+        when_inside(n, lambda n=n: to(n).start())
 
     highest = lax.Precision.HIGHEST
     for fetch in fetches[3:]:
@@ -200,8 +214,8 @@
     store(up_v, up_h)
     store(weight, weight_out_h)
 
-    for copy in copies:
-        copy.wait_recv()
+    for n in others:
+        when_inside(26 - n, lambda n=n: to(n).wait_recv())
     store(halo, halo_h)
 
     for ref, k in ((near_s, 0), (code_s, 1), (far_s, 2)):
@@ -247,8 +261,8 @@
     store(table, table_h)
     for copy in stores:
         copy.wait()
-    for copy in copies:
-        copy.wait_send()
+    for n in others:
+        when_inside(n, lambda n=n: to(n).wait_send())
 
 
 def sums_kernel(

time: 54 us -> 50 us (0.926)
  the two profiles are of different devices: /device:TPU:152 before, /device:TPU:197 now
where the time goes in v4:
time: 50 us; the launch traced here: 49.9 us
  Pallas kernels  49.2 us (98%)
  between operations  0.66 us (1%)
    pallas_call x1, Pallas kernels, sums(): pl.pallas_call(sums_kernel, out_shape=jax.ShapeDtypeStruct((3, CELLS, POI...  38.8 us
    pallas_call x1, Pallas kernels, shards(): pl.pallas_call(exchange_kernel, out_shape=[jax.ShapeDtypeStruct(*h) for h...  10.4 us

profile of v4, /device:TPU:197, one launch (start us, length us, event | category | flops | bytes accessed | tf_op | source)
XLA Modules:
  0.0 49.9 jit_solution(12392135514597622020)
XLA Ops:
  0.7 10.4 %exchange.1 = (f32[108,8,128]{2,1,0:T(8,128)}, s32[2,512]{1,0:T(2,128)}, bf16[4,3,208,128]{3,2,1,0:T(8,128)(2,1)}, f32[2,16,384]{2,1,0:T(8,128)}, bf16[768,384]{...) custom-call(s32[1,1,1]{2,1,0:T(1,128)S(6)} %copy.9.count_h, f32[3,4,312]{2,1,0:T(4,128)} %bitcast.12, ...), custom_call_target="tpu_custom_call" | custom-call | tf_op jit(solution)/shard_map/exchange/pallas_call | solution.py:430
  11.0 38.8 %sums.1 = f32[3,4,312]{2,1,0:T(4,128)} custom-call(s32[2,512]{1,0:T(2,128)} %get-tuple-element.12.table_h, f32[108,8,128]{2,1,0:T(8,128)} %get-tuple-element.13.halo_h, bf16[4,3,208,128]{3,2,1,0:T(8,128)(2,1)} %get-tuple-element.14.target_h, f32[2,16,384]{2,1,0:T(8,128)} %get-tuple-element.15.own_h, bf16[768,384]{1,0:T(8,128)(2,1)} %get-tuple-element.16.bend_h, ...), custom_call_target="tpu_custom_call" | custom-call | tf_op jit(solution)/shard_map/sums/pallas_call | solution.py:405

commit v5 on v4

--- a/solution.py
+++ b/solution.py
@@ -282,10 +282,17 @@
     wide_s, forms_s = (wide0, wide1), (forms0, forms1)
     total_s[...] = jnp.zeros(total_s.shape, F32)
     source_s[...] = jnp.zeros(source_s.shape, F32)
-    for fetch in fetches:
-        fetch.wait()
+    fetches[0].wait()
+    fetches[1].wait()
     count = table[1, 0]
     row8 = lax.broadcasted_iota(jnp.int32, (8, RW), 0)
+
+    def arrive(g, *which):
+        def wait():
+            for i in which:
+                fetches[i].wait()
+
+        pl.when(g == 0)(wait)
 
     def group(g, carry):
         first = g * GROUP
@@ -299,8 +306,10 @@
             source_s[e // 2, at_row : at_row + 1, 2 * LANES :] = tile[6:7]
             source_s[e // 2, at_row + 1 : at_row + 2, 2 * LANES :] = pltpu.roll(tile[6:7], 64, 1)
             source_s[e // 2, at_row + 2 : at_row + 3, 2 * LANES :] = tile[7:8]
+        arrive(g, 2)
         places = split_rows(source_s[...].reshape(GROUP * 4, PW))
         bent = split_rows(split_dot(places, bend))
+        arrive(g, 3, 4, 5)
         raised = split_dot(jnp.concatenate([places, bent], axis=0), up)
         raised_s[...] = raised.reshape(2, GROUP // 2, 8, RW)
 
@@ -348,7 +357,8 @@
         def two(i, carry):
             for half in range(2):
                 e = 2 * i + half
-                cell = jnp.where(e < last - first, cell_of(e), CELLS)
+                cell = cell_of(e)
+                turns = jnp.where(e < last - first, CHUNKS, 0) if half else CHUNKS
                 later = cell_of(e + 1)
                 prepare(i + half, 1 - half, 1 - half)
 
@@ -358,7 +368,7 @@
                         fold(cell, half, q, begin, min(3, CHUNK // 8 - begin))
                     return carry
 
-                lax.fori_loop(0, CHUNKS, chunk, 0)
+                lax.fori_loop(0, turns, chunk, 0)
             return carry
 
         prepare(0, 0, 0)
@@ -369,21 +379,18 @@
 
     lax.fori_loop(0, (count + GROUP - 1) // GROUP, group, 0)
 
-    ones = jnp.ones((8, LANES), BF16)
-
-    def reduced(x):
-        high, low = split2(x)
-        return (dot_nt(ones, high) + dot_nt(ones, low))[0:1, :]
-
+    fetches[6].wait()
+    ones = jnp.ones((8, 2 * LANES), BF16)
     for c in range(CELLS):
-        weight_sum = reduced(total_s[c, 3].reshape(POINTS, LANES))
+        split = jnp.concatenate(split2(total_s[c].reshape(4 * POINTS, LANES)), axis=1)
+        summed = dot_nt(ones, split)[0:1, :]
+        parts = [summed[:, k * POINTS : (k + 1) * POINTS] for k in range(4)]
         for k in range(3):
             row = 4 * c + k
-            place = own[0, row : row + 1, :POINTS]
             velocity[k, c : c + 1, :] = (
                 0.25 * own[1, row : row + 1, :POINTS]
-                + reduced(total_s[c, k].reshape(POINTS, LANES))
-                + place * weight_sum
+                + parts[k]
+                + own[0, row : row + 1, :POINTS] * parts[3]
             )
 
 
@@ -418,7 +425,7 @@
             pltpu.VMEM((6, 8, RW), F32),
             pltpu.VMEM((CHUNKS, 2 * CHUNK, RW), F32),
             pltpu.VMEM((CHUNKS, 2 * CHUNK, RW), F32),
-            pltpu.VMEM((CELLS + 1, 4, CHUNKS, CHUNK, LANES), F32),
+            pltpu.VMEM((CELLS, 4, CHUNKS, CHUNK, LANES), F32),
             pltpu.VMEM((DEPTH, RW), BF16),
         ],
         compiler_params=pltpu.CompilerParams(vmem_limit_bytes=VMEM_BYTES),

time: 50 us -> 48.5 us (0.970)
  the two profiles are of different devices: /device:TPU:197 before, /device:TPU:97 now
where the time goes in v5:
time: 48.5 us; the launch traced here: 48.2 us
  Pallas kernels  47.5 us (98%)
  between operations  0.66 us (1%)
    pallas_call x1, Pallas kernels, sums(): pl.pallas_call(sums_kernel, out_shape=jax.ShapeDtypeStruct((3, CELLS, POI...  36.2 us
    pallas_call x1, Pallas kernels, shards(): pl.pallas_call(exchange_kernel, out_shape=[jax.ShapeDtypeStruct(*h) for h...  11.3 us

profile of v5, /device:TPU:97, one launch (start us, length us, event | category | flops | bytes accessed | tf_op | source)
XLA Modules:
  0.0 48.2 jit_solution(4466290036250236750)
XLA Ops:
  0.7 11.3 %exchange.1 = (f32[108,8,128]{2,1,0:T(8,128)}, s32[2,512]{1,0:T(2,128)}, bf16[4,3,208,128]{3,2,1,0:T(8,128)(2,1)}, f32[2,16,384]{2,1,0:T(8,128)}, bf16[768,384]{...) custom-call(s32[1,1,1]{2,1,0:T(1,128)S(6)} %copy.9.count_h, f32[3,4,312]{2,1,0:T(4,128)} %bitcast.12, ...), custom_call_target="tpu_custom_call" | custom-call | tf_op jit(solution)/shard_map/exchange/pallas_call | solution.py:437
  12.0 36.2 %sums.1 = f32[3,4,312]{2,1,0:T(4,128)} custom-call(s32[2,512]{1,0:T(2,128)} %get-tuple-element.12.table_h, f32[108,8,128]{2,1,0:T(8,128)} %get-tuple-element.13.halo_h, bf16[4,3,208,128]{3,2,1,0:T(8,128)(2,1)} %get-tuple-element.14.target_h, f32[2,16,384]{2,1,0:T(8,128)} %get-tuple-element.15.own_h, bf16[768,384]{1,0:T(8,128)(2,1)} %get-tuple-element.16.bend_h, ...), custom_call_target="tpu_custom_call" | custom-call | tf_op jit(solution)/shard_map/sums/pallas_call | solution.py:412
